TPU v7x, 512 devices: a whole 4x8x8 slice. The times are simulated.
512 devices in a mesh: slab: 16 (over y, core), plane: 32 (over x, z).
Axes of the slice: x: 4, y: 8, z: 8, core: 2. Of those that a mesh axis runs over, the one named last changes fastest.
Arguments:
- features: float32 [32, 48, 128, 1024], P(None, 'slab', 'plane'), may hold values from -6 to 6
- x_taps: float32 [32, 31], replicated, may hold values from -1 to 1
- y_taps: float32 [32, 31], replicated, may hold values from -1 to 1
- expand: bfloat16 [128, 32], replicated, may hold values from -1 to 1
- expand_bias: float32 [128], replicated, may hold values from -4 to 4
- project: bfloat16 [32, 128], replicated, may hold values from -0.5 to 0.5
- atlas_tiles: bfloat16 [128, 32, 2048], P('slab'), may hold values from -6 to 6
- footprint: int32 [16, 32], P('slab'), may hold values from -1 to 127, as said below
- block_slot: int32 [48, 128, 2], P('slab', 'plane'), may hold values from 0 to 31, as said below
- tile_base: int32 [3, 48, 128, 2], P(None, 'slab', 'plane'), may hold values from 0 to 7, as said below
- displacement: float32 [3, 48, 128, 1024], P(None, 'slab', 'plane'), may hold values from -1 to 9
Outputs:
- output: float32 [32, 48, 128, 1024], P(None, 'slab', 'plane')
Inputs may be any that keep to these rules, and one draw needn't show every extreme that they name: `footprint`: entry o * 2 + k of row g is -1 or an atlas tile owned by slab group o, a number from o * 8 to (o + 1) * 8 - 1; within each aligned block of 2 entries the -1 entries come last; entries g * 2 to (g + 1) * 2 - 1 of row g are never -1. `block_slot`: each block names an entry of its slab group's row of footprint that is not -1. `tile_base`: component 0 is below 4; components 1 and 2 are below 8.
All inputs are finite; a program needn't handle non-finite values.
Results may differ from a plain program's by a relative error of at most 0.0027.
Values may be sent and summed in bfloat16 or wider, within the bound.
A program may use at most 128 MiB of HBM per device.

v0:
```python
import jax
import jax.numpy as jnp
from jax import lax
from jax.sharding import PartitionSpec as P

TZ = 8
TY = 16
TX = 16
BLK = 512


def gelu_tanh(values):
    return (
        0.5
        * values
        * (1.0 + jnp.tanh(0.7978845608028654 * (values + 0.044715 * values * values * values)))
    )


def taps_valid(padded, taps, axis, length):
    total = jnp.zeros(padded.shape[:axis] + (length,) + padded.shape[axis + 1 :], jnp.float32)
    for offset in range(taps.shape[1]):
        window = lax.slice_in_dim(padded, offset, offset + length, axis=axis)
        total = total + taps[:, offset].reshape((-1,) + (1,) * (padded.ndim - 1)) * window
    return total


def depthwise(field, taps, axis):
    half_taps = taps.shape[1] // 2
    padding = [(0, 0)] * field.ndim
    padding[axis] = (half_taps, half_taps)
    return taps_valid(jnp.pad(field, padding), taps, axis, field.shape[axis])


def tent_table(place, cells):
    clipped = jnp.clip(place, 0.0, cells - 1.0)
    grid = jnp.arange(cells, dtype=jnp.float32)[:, None]
    return jnp.maximum(0.0, 1.0 - jnp.abs(clipped[None, :] - grid))


def body(
    features,
    x_taps,
    y_taps,
    expand,
    expand_bias,
    project,
    atlas_tiles,
    footprint,
    block_slot,
    tile_base,
    displacement,
):
    channels, z_rows, y_rows, x_cells = features.shape
    xconv = depthwise(features, x_taps, 3)
    filtered = depthwise(
        lax.all_to_all(xconv, "plane", split_axis=3, concat_axis=2, tiled=True), y_taps, 2
    )
    yconv = lax.all_to_all(
        filtered.astype(jnp.bfloat16), "plane", split_axis=2, concat_axis=3, tiled=True
    ).astype(filtered.dtype)
    mixed_in = yconv.astype(jnp.bfloat16).reshape(channels, -1)
    hidden = gelu_tanh(
        jnp.dot(expand, mixed_in, preferred_element_type=jnp.float32) + expand_bias[:, None]
    ).astype(jnp.bfloat16)
    mlp_out = jnp.dot(project, hidden, preferred_element_type=jnp.float32).reshape(features.shape)
    slab_count = lax.axis_size("slab")
    capacity = footprint.shape[1] // slab_count
    requests = footprint.reshape(slab_count, capacity)
    requested = lax.all_to_all(requests, "slab", split_axis=0, concat_axis=0, tiled=True)
    tiles_held = atlas_tiles.shape[0]
    tile_cells = atlas_tiles.shape[2]
    local_ids = requested - lax.axis_index("slab") * tiles_held
    selector = (
        local_ids.reshape(-1, 1) == jnp.arange(tiles_held, dtype=jnp.int32)[None, :]
    ).astype(jnp.bfloat16)
    picked = jnp.dot(
        selector, atlas_tiles.reshape(tiles_held, -1), preferred_element_type=jnp.float32
    ).astype(jnp.bfloat16)
    fetched = lax.all_to_all(
        picked.reshape(slab_count, capacity, channels, tile_cells),
        "slab",
        split_axis=0,
        concat_axis=0,
        tiled=True,
    )
    library = fetched.reshape(slab_count * capacity, channels, tile_cells)
    block_count = z_rows * y_rows * (x_cells // BLK)
    shifts = displacement.reshape(3, block_count, BLK)
    bases = tile_base.reshape(3, block_count, 1).astype(jnp.float32)
    positions = (bases + shifts).transpose(1, 0, 2)
    slots = block_slot.reshape(block_count)

    def sample(item):
        slot, place = item
        tile = lax.dynamic_index_in_dim(library, slot, 0, keepdims=False)
        weight_z = tent_table(place[0], TZ)
        weight_y = tent_table(place[1], TY)
        weight_x = tent_table(place[2], TX)
        interp = (
            (weight_z[:, None, None, :] * weight_y[None, :, None, :] * weight_x[None, None, :, :])
            .reshape(-1, place.shape[1])
            .astype(jnp.bfloat16)
        )
        return jnp.dot(tile, interp, preferred_element_type=jnp.float32)

    sampled = lax.map(sample, (slots, positions))
    warped = (
        sampled.reshape(z_rows, y_rows, -1, channels, BLK)
        .transpose(3, 0, 1, 2, 4)
        .reshape(channels, z_rows, y_rows, x_cells)
    )
    return features + mlp_out + warped


def solution(mesh):
    return jax.shard_map(
        body,
        mesh=mesh,
        in_specs=(
            P(None, "slab", "plane", None),
            P(),
            P(),
            P(),
            P(),
            P(),
            P("slab", None, None),
            P("slab", None),
            P("slab", "plane", None),
            P(None, "slab", "plane", None),
            P(None, "slab", "plane", None),
        ),
        out_specs=P(None, "slab", "plane", None),
        check_vma=False,
    )
```

profile of v0, /device:TPU:1, one launch (start us, length us, event | category | flops | bytes accessed | tf_op | source)
XLA Modules:
  0.0 412.4 jit_solution(7294122362549979353)
XLA Ops:
  0.0 2.5 slice_reduce_fusion.60
  4.3 2.3 copy.44
  6.7 12.7 %fusion.66 = f32[32,3,4,1024]{3,0,2,1:T(8,128)S(1)} fusion(f32[32,3,4,1024]{3,0,2,1:T(8,128)S(1)} %copy.44, f32[32]{0:T(128)S(1)} %get-tuple-element.113, f32[32]{0:T(128)S(1)} %get-tuple-element.114, f32[32]{0:T(128)S(1)} %get-tuple-element.85, f32[32]{0:T(128)S(1)} %get-tuple-element.86, f32[32]{0:T(128)S(1)} %get-tuple-element.87, ...), kind=kLoop, calls=%fused_computation.140 | loop fusion | flops 23986176 | bytes 3149696 | tf_op jit(solution)/shard_map/add | solution.py:24
  19.4 4.7 %copy.46 = f32[32,3,4,1024]{0,2,1,3:T(4,128)} copy(f32[32,3,4,1024]{3,0,2,1:T(8,128)S(1)} %fusion.66) | data formatting | bytes 3145728 | tf_op jit(solution)/shard_map/add | solution.py:24
  24.1 6.8 %reshape.312 = f32[32,1,12288]{2,1,0:T(1,128)} reshape(f32[1024,3,4,32]{3,2,1,0:T(4,128)} %bitcast.85) | data formatting | bytes 3145728
  30.8 13.8 %all-to-all-start = ((f32[32,1,12288]{2,1,0:T(1,128)}), f32[32,1,12288]{2,1,0:T(1,128)S(1)}, u32[]{:S(2)}, u32[]{:S(2)}) async-start(f32[32,1,12288]{2,1,0:T(1,128)} %reshape.312), calls=%async_computation | async-start | bytes 3145728 | tf_op jit(solution)/shard_map/all_to_all | solution.py:57
  47.6 33.9 %all-to-all-done = f32[32,1,12288]{2,1,0:T(1,128)S(1)} async-done(((f32[32,1,12288]{2,1,0:T(1,128)}), f32[32,1,12288]{2,1,0:T(1,128)S(1)}, u32[]{:S(2)}, u32[]{:S(2)}) %all-to-all-start) | async-done | bytes 1572896 | tf_op jit(solution)/shard_map/all_to_all | solution.py:57
  81.5 10.9 %all-to-all-start.2 = ((s32[16,1,2]{2,1,0:T(1,128)}), s32[16,1,2]{2,1,0:T(1,128)S(1)}, u32[]{:S(2)}, u32[]{:S(2)}) async-start(s32[16,1,2]{2,1,0:T(1,128)} %bitcast.15), calls=%async_computation.2 | async-start | bytes 16384 | tf_op jit(solution)/shard_map/all_to_all | solution.py:70
  93.0 4.6 %reduce.132 = f32[32,12288]{1,0:T(8,128)S(1)} reduce(f32[32,1,12288]{2,1,0:T(1,128)S(1)} %all-to-all-done, f32[]{:T(128)} %broadcast.213), dimensions={1}, to_apply=%all_to_all.33.reduce_sub_computation | reduce | bytes 3145732 | tf_op jit(solution)/shard_map/all_to_all | solution.py:57
  97.6 4.9 %reshape.313 = f32[1024,3,4,32]{3,2,1,0:T(4,128)} reshape(f32[32,12288]{1,0:T(8,128)S(1)} %reduce.132) | data formatting | bytes 3145728
  102.5 7.6 %copy.47 = f32[32,3,4,32,32]{4,0,2,3,1:T(8,128)} copy(f32[32,3,4,32,32]{0,2,1,4,3:T(4,128)} %bitcast.83) | data formatting | bytes 3145728 | tf_op jit(solution)/shard_map/all_to_all | solution.py:57
  110.0 5.3 %copy.48 = f32[32,3,128,32]{2,3,1,0:T(8,128)S(1)} copy(f32[32,3,128,32]{3,0,2,1:T(8,128)} %bitcast.84) | data formatting | bytes 3145728 | tf_op jit(solution)/shard_map/all_to_all | solution.py:57
  115.4 16.0 %fusion.126 = bf16[32,3,128,32]{2,3,1,0:T(8,128)(2,1)} fusion(f32[32,3,128,32]{2,3,1,0:T(8,128)S(1)} %copy.48, f32[32]{0:T(128)S(1)} %get-tuple-element.82, f32[32]{0:T(128)S(1)} %get-tuple-element.83, f32[32]{0:T(128)S(1)} %get-tuple-element.54, f32[32]{0:T(128)S(1)} %get-tuple-element.55, f32[32]{0:T(128)S(1)} %get-tuple-element.56, ...), kind=kLoop, calls=%fused_computation.200 | loop fusion | flops 24379392 | bytes 2363264 | tf_op jit(solution)/shard_map/convert_element_type | solution.py:60
  131.4 5.3 %copy.50 = bf16[32,3,128,32]{3,0,1,2:T(8,128)(2,1)S(1)} copy(bf16[32,3,128,32]{2,3,1,0:T(8,128)(2,1)} %fusion.126) | data formatting | bytes 1572864 | tf_op jit(solution)/shard_map/convert_element_type | solution.py:60
  136.7 15.2 %reshape.314 = bf16[32,2,6144]{2,1,0:T(2,128)(2,1)} reshape(bf16[128,3,32,32]{3,2,1,0:T(8,128)(2,1)S(1)} %bitcast.90) | data formatting | bytes 1572864
  151.9 5.5 %all-to-all-start.1 = ((bf16[32,2,6144]{2,1,0:T(2,128)(2,1)}), bf16[32,2,6144]{2,1,0:T(2,128)(2,1)S(1)}, u32[]{:S(2)}, u32[]{:S(2)}) async-start(bf16[32,2,6144]{2,1,0:T(2,128)(2,1)} %reshape.314), calls=%async_computation.1 | async-start | bytes 1572864 | tf_op jit(solution)/shard_map/all_to_all | solution.py:59
  159.3 4.3 %copy.62 = bf16[4,8,32,2048]{3,2,1,0:T(8,128)(2,1)} copy(bf16[4,8,32,2048]{3,1,2,0:T(8,128)(2,1)S(1)} %bitcast.87) | data formatting | bytes 8388608
  163.6 14.1 %all-to-all-done.1 = bf16[32,2,6144]{2,1,0:T(2,128)(2,1)S(1)} async-done(((bf16[32,2,6144]{2,1,0:T(2,128)(2,1)}), bf16[32,2,6144]{2,1,0:T(2,128)(2,1)S(1)}, u32[]{:S(2)}, u32[]{:S(2)}) %all-to-all-start.1) | async-done | bytes 786464 | tf_op jit(solution)/shard_map/all_to_all | solution.py:59
  178.6 10.0 %all-to-all-start.3 = ((bf16[16,2,32,2048]{3,2,1,0:T(8,128)(2,1)}), bf16[16,2,32,2048]{3,2,1,0:T(8,128)(2,1)}, u32[]{:S(2)}, u32[]{:S(2)}) async-start(bf16[16,2,32,2048]{3,2,1,0:T(8,128)(2,1)} %bitcast.86), calls=%async_computation.3 | async-start | bytes 8388608 | tf_op jit(solution)/shard_map/all_to_all | solution.py:80
  189.3 4.0 reshape.315
  193.3 3.8 copy.65
  197.1 4.8 %reshape.227 = bf16[32,12288]{1,0:T(8,128)(2,1)S(1)} reshape(bf16[32,3,4,32,32]{4,3,2,1,0:T(8,128)(2,1)} %bitcast.89) | data formatting | bytes 1572864 | tf_op jit(solution)/shard_map/reshape | solution.py:62
  201.9 2.6 convolution_bitcast_fusion.1
  204.5 2.3 reshape.228
  206.8 75.4 %all-to-all-done.3 = bf16[16,2,32,2048]{3,2,1,0:T(8,128)(2,1)} async-done(((bf16[16,2,32,2048]{3,2,1,0:T(8,128)(2,1)}), bf16[16,2,32,2048]{3,2,1,0:T(8,128)(2,1)}, u32[]{:S(2)}, u32[]{:S(2)}) %all-to-all-start.3) | async-done | bytes 4194336 | tf_op jit(solution)/shard_map/all_to_all | solution.py:80
  282.3 120.4 %while.10 = (s32[]{:T(128)}, f32[24,32,512]{2,1,0:T(8,128)}, s32[24]{0:T(128)S(1)}, bf16[32,32,2048]{2,1,0:T(8,128)(2,1)}, f32[24,3,512]{2,0,1:T(8,128)S(1)}, /*...) while((s32[]{:T(128)}, f32[24,32,512]{2,1,0:T(8,128)}, s32[24]{0:T(128)S(1)}, ...), condition=%wide.region_1.2_spmd, body=%wide.region_0.1_spmd.sunk | while | flops 69355016 | bytes 5098171 | solution.py:107
  295.3 2.0 fusion.151
  310.3 2.0 fusion.151
  315.3 2.0 fusion.151
  402.7 2.6 copy.66
  405.3 2.8 reshape.235
  408.1 4.1 %add_add_fusion = f32[32,3,4,1024]{3,2,1,0:T(4,128)} fusion(f32[32,3,4,1024]{3,2,1,0:T(4,128)} %reshape.235, f32[32,3,4,1024]{3,2,1,0:T(4,128)S(1)} %copy-done.2, f32[32,3,4,1024]{3,2,1,0:T(4,128)} %reshape.228), kind=kLoop, calls=%fused_computation.209 | loop fusion | flops 786432 | bytes 6291456 | tf_op jit(solution)/shard_map/add | solution.py:113
  (231 shorter events, 82.6 us)
Async XLA Ops:
  0.0 201.9 %copy-start = (bf16[32,128]{1,0:T(8,128)(2,1)S(1)}, bf16[32,128]{1,0:T(8,128)(2,1)}, u32[]{:S(2)}) copy-start(bf16[32,128]{1,0:T(8,128)(2,1)} %param.18) | copy-start | bytes 24580
  30.8 14.5 %copy-start.9 = (s32[1,32]{1,0:T(1,128)S(1)}, s32[1,32]{1,0:T(1,128)}, u32[]{:S(2)}) copy-start(s32[1,32]{1,0:T(1,128)} %param.20) | copy-start | bytes 388
  30.8 15.8 %copy-start.1 = (f32[32,31]{1,0:T(8,128)S(1)}, f32[32,31]{1,0:T(8,128)}, u32[]{:S(2)}) copy-start(f32[32,31]{1,0:T(8,128)} %param.15) | copy-start | bytes 11908
  30.8 50.7 %all-to-all-start = ((f32[32,1,12288]{2,1,0:T(1,128)}), f32[32,1,12288]{2,1,0:T(1,128)S(1)}, u32[]{:S(2)}, u32[]{:S(2)}) async-start(f32[32,1,12288]{2,1,0:T(1,128)} %reshape.312), calls=%async_computation | async-start | bytes 3145728 | tf_op jit(solution)/shard_map/all_to_all | solution.py:57
  81.5 70.4 %all-to-all-start.2 = ((s32[16,1,2]{2,1,0:T(1,128)}), s32[16,1,2]{2,1,0:T(1,128)S(1)}, u32[]{:S(2)}, u32[]{:S(2)}) async-start(s32[16,1,2]{2,1,0:T(1,128)} %bitcast.15), calls=%async_computation.2 | async-start | bytes 16384 | tf_op jit(solution)/shard_map/all_to_all | solution.py:70
  151.9 5.5 %copy-start.4 = (bf16[8,32,2048]{2,1,0:T(8,128)(2,1)S(1)}, bf16[8,32,2048]{2,1,0:T(8,128)(2,1)}, u32[]{:S(2)}) copy-start(bf16[8,32,2048]{2,1,0:T(8,128)(2,1)} %param.19) | copy-start | bytes 3145732
  151.9 25.8 %all-to-all-start.1 = ((bf16[32,2,6144]{2,1,0:T(2,128)(2,1)}), bf16[32,2,6144]{2,1,0:T(2,128)(2,1)S(1)}, u32[]{:S(2)}, u32[]{:S(2)}) async-start(bf16[32,2,6144]{2,1,0:T(2,128)(2,1)} %reshape.314), calls=%async_computation.1 | async-start | bytes 1572864 | tf_op jit(solution)/shard_map/all_to_all | solution.py:59
  177.7 0.9 copy-start.3
  177.7 11.0 %copy-start.5 = (f32[3,3,4,1024]{3,2,1,0:T(4,128)S(1)}, f32[3,3,4,1024]{3,2,1,0:T(4,128)}, u32[]{:S(2)}) copy-start(f32[3,3,4,1024]{3,2,1,0:T(4,128)} %param.23) | copy-start | bytes 442372
  177.7 11.1 %copy-start.6 = (s32[3,3,4,2]{2,3,1,0:T(2,128)S(1)}, s32[3,3,4,2]{2,3,1,0:T(2,128)}, u32[]{:S(2)}) copy-start(s32[3,3,4,2]{2,3,1,0:T(2,128)} %param.22) | copy-start | bytes 868
  177.7 11.3 %copy-start.7 = (s32[3,4,2]{1,2,0:T(2,128)S(1)}, s32[3,4,2]{1,2,0:T(2,128)}, u32[]{:S(2)}) copy-start(s32[3,4,2]{1,2,0:T(2,128)} %param.21) | copy-start | bytes 292
  178.6 103.6 %all-to-all-start.3 = ((bf16[16,2,32,2048]{3,2,1,0:T(8,128)(2,1)}), bf16[16,2,32,2048]{3,2,1,0:T(8,128)(2,1)}, u32[]{:S(2)}, u32[]{:S(2)}) async-start(bf16[16,2,32,2048]{3,2,1,0:T(8,128)(2,1)} %bitcast.86), calls=%async_computation.3 | async-start | bytes 8388608 | tf_op jit(solution)/shard_map/all_to_all | solution.py:80
  197.1 4.8 %copy-start.8 = (bf16[128,32]{0,1:T(8,128)(2,1)S(1)}, bf16[128,32]{0,1:T(8,128)(2,1)}, u32[]{:S(2)}) copy-start(bf16[128,32]{0,1:T(8,128)(2,1)} %param.16) | copy-start | bytes 24580
  197.1 4.8 %copy-start.10 = (f32[128]{0:T(128)S(1)}, f32[128]{0:T(128)}, u32[]{:S(2)}) copy-start(f32[128]{0:T(128)} %param.17) | copy-start | bytes 1540
  405.3 2.8 copy-start.2
where the time goes:
time: 415 us; the launch traced here: 412 us
  waiting for transfers between devices  123 us (30%)
  local copies, waits for them, and re-layouts  99.2 us (24%)
  other arithmetic  56.6 us (14%)
  matrix products  52 us (13%)
  loops' own time  40.5 us (10%)
  starting transfers between devices  40.3 us (10%)
    all_to_all x1, waiting for transfers between devices, body(): lax.all_to_all(picked.reshape(slab_count, capacity, channels, tile_cells)...  75.4 us
    dot_general x24, matrix products, sample(): return jnp.dot(tile, interp, preferred_element_type=jnp.float32)  48.1 us
    another operation x1, loops' own time, body(): sampled = lax.map(sample, (slots, positions))  40.5 us
    unnamed x31, local copies, waits for them, and re-layouts  39.7 us
    all_to_all x1, waiting for transfers between devices, body(): lax.all_to_all(xconv, 'plane', split_axis=3, concat_axis=2, tiled=True)  33.9 us
    convert_element_type x24, other arithmetic, sample(): interp = (weight_z[:, None, None, :] * weight_y[None, :, None, :] * weigh...  16.6 us
    convert_element_type x1, other arithmetic, body(): filtered.astype(jnp.bfloat16)  16 us
    all_to_all x1, waiting for transfers between devices, body(): lax.all_to_all(filtered.astype(jnp.bfloat16), 'plane', split_axis=2, conc...  14.1 us
  transfers between devices with their start and end apart: 4, of which 3 were waited for; matrix products, arithmetic and copies ran while one was open for 21% of the time, Pallas kernels for 0%

commit v1 on v0

v1 whole, which is shorter than its diff:
```python
import functools

import jax
import jax.numpy as jnp
from jax import lax
from jax.experimental import pallas as pl
from jax.experimental.pallas import tpu as pltpu
from jax.sharding import PartitionSpec as P

TZ = 8
TY = 16
TX = 16
BLK = 512
KZ = 8
KX = 4
NP = KX * KZ
NS = 16
CAP = 2
SLOTS = NS * CAP
HELD = 8
ZD = 3
YR = 4
XQ = 4
QW = 256
ROWS = XQ * YR
F32 = jnp.float32
BF16 = jnp.bfloat16
MESH = pl.DeviceIdType.MESH


def dot(a, b):
    return jnp.dot(a, b, preferred_element_type=F32)


def split2(value):
    high = value.astype(BF16)
    return high, (value - high.astype(F32)).astype(BF16)


def exchange_kernel(
    feat_ref,
    xt_ref,
    yt_ref,
    fp_ref,
    atlas_ref,
    mixed_ref,
    lib_ref,
    feat,
    chunks,
    cols,
    back,
    pieces,
    picked,
    bm,
    tx,
    in_sem,
    a_send,
    a_recv,
    b_send,
    b_recv,
    b_own,
    y_send,
    y_recv,
    g_own,
    g_send,
    g_recv,
):
    s = lax.axis_index("slab")
    p = lax.axis_index("plane")
    px = p // KZ
    pz = lax.rem(p, KZ)

    loads = [
        pltpu.make_async_copy(feat_ref.at[:, z], feat.at[z], in_sem.at[z]) for z in range(ZD)
    ]
    half = p // 16
    cell = lax.rem(p, 16)
    atlas_load = pltpu.make_async_copy(
        atlas_ref.at[:, pl.ds(half * 16, 16), pl.ds(pl.multiple_of(cell * 128, 128), 128)],
        pieces.at[pl.ds(s * HELD, HELD)],
        in_sem.at[ZD],
    )
    atlas_load.start()
    for load in loads:
        load.start()

    barrier = pltpu.get_barrier_semaphore()

    def greet_plane(i, carry):
        pl.semaphore_signal(
            barrier, inc=1, device_id={"plane": lax.rem(p + i, NP)}, device_id_type=MESH
        )
        return carry

    def greet_slab(i, carry):
        pl.semaphore_signal(
            barrier, inc=1, device_id={"slab": lax.rem(s + i, NS)}, device_id_type=MESH
        )
        return carry

    lax.fori_loop(1, NP, greet_plane, 0)
    lax.fori_loop(1, NS, greet_slab, 0)

    def make_chunks(z):
        loads[z].wait()

        def step(c, carry):
            block = feat[z, c]
            stacked = jnp.concatenate(
                [block[:, q * QW : (q + 1) * QW] for q in range(XQ)], axis=0
            )
            chunks[z, c] = stacked.astype(BF16)
            return carry

        lax.fori_loop(0, NP, step, 0)

    def send_chunks(z):
        def step(i, carry):
            peer = lax.rem(p + i, NP)
            pltpu.make_async_remote_copy(
                chunks.at[z, peer],
                cols.at[z, p],
                a_send.at[z],
                a_recv.at[z],
                device_id={"plane": peer},
                device_id_type=MESH,
            ).start()
            return carry

        lax.fori_loop(1, NP, step, 0)
        cols[z, p] = chunks[z, p]

    make_chunks(0)
    atlas_load.wait()
    pl.semaphore_wait(barrier, NP - 1 + NS - 1)

    def send_piece(i, carry):
        peer = lax.rem(s + i, NS)
        pltpu.make_async_remote_copy(
            pieces.at[pl.ds(s * HELD, HELD)],
            pieces.at[pl.ds(s * HELD, HELD)],
            y_send,
            y_recv,
            device_id={"slab": peer},
            device_id_type=MESH,
        ).start()
        return carry

    lax.fori_loop(1, NS, send_piece, 0)
    send_chunks(0)
    for z in range(1, ZD):
        make_chunks(z)
        send_chunks(z)

    size = NP * ROWS

    def taps_at(index, ref):
        total = jnp.zeros(index.shape, F32)
        for t in range(31):
            total = jnp.where(index == t, ref[p, t], total)
        return total

    def build_rows(m, carry):
        out = lax.broadcasted_iota(jnp.int32, (64, size), 0) + m * 64
        inp = lax.broadcasted_iota(jnp.int32, (64, size), 1)
        row = lambda r: lax.shift_right_logical(r, 4) * 4 + (r & 3)
        quarter = lambda r: lax.shift_right_logical(r, 2) & 3
        weights = taps_at(row(inp) - row(out) + 15, yt_ref)
        for n, shift in enumerate((0, -1, 1)):
            kept = jnp.where(quarter(inp) == quarter(out) + shift, weights, 0.0)
            high, low = split2(kept)
            bm[2 * n, pl.ds(m * 64, 64)] = high
            bm[2 * n + 1, pl.ds(m * 64, 64)] = low
        return carry

    lax.fori_loop(0, size // 64, build_rows, 0)

    def build_x(m, carry):
        k = lax.broadcasted_iota(jnp.int32, (64, QW), 0) + m * 64
        n = lax.broadcasted_iota(jnp.int32, (64, QW), 1)
        high, low = split2(taps_at(k - 128 - n + 15, xt_ref))
        tx[0, pl.ds(m * 64, 64)] = high
        tx[1, pl.ds(m * 64, 64)] = low
        return carry

    lax.fori_loop(0, 8, build_x, 0)

    wait_all = lambda ref, sem: pltpu.make_async_copy(ref, ref, sem).wait()
    wait_all(pieces.at[pl.ds(0, (NS - 1) * HELD)], y_recv)

    def pick(slot, carry):
        tile = jnp.maximum(fp_ref[0, slot], 0)
        picked[slot] = pieces[tile]
        return carry

    lax.fori_loop(0, SLOTS, pick, 0)

    sends = []

    def pass_on(source, target, count, device, sem, index):
        copy = pltpu.make_async_remote_copy(
            source,
            target,
            g_send.at[len(sends)],
            g_recv.at[index],
            device_id={"plane": device},
            device_id_type=MESH,
        )
        copy.start()
        sends.append(copy)
        return copy

    at = lambda x, z: lax.rem(x + KX, KX) * KZ + lax.rem(z + KZ, KZ)
    up, down = at(px, pz + 1), at(px, pz - 1)
    right, left = at(px + 1, pz), at(px - 1, pz)
    first, second = pl.ds(0, SLOTS // 2), pl.ds(SLOTS // 2, SLOTS // 2)
    recv = {}

    def spread(dz, source, target):
        index = dz + 3
        recv["r", dz] = pass_on(source, target, SLOTS, right, g_recv, 7 + index)
        recv["l", dz] = pass_on(source, target, SLOTS, left, g_recv, 15 + index)

    own = lib_ref.at[p]
    recv["u", 1] = pass_on(picked, own, SLOTS, up, g_recv, 0)
    recv["d", 1] = pass_on(picked, own, SLOTS, down, g_recv, 4)
    spread(0, picked, own)
    own_copy = pltpu.make_async_copy(picked, own, g_own)
    own_copy.start()

    def z_step(r):
        recv["u", r].wait_recv()
        piece = lib_ref.at[at(px, pz - r)]
        if r < 4:
            recv["u", r + 1] = pass_on(piece, piece, SLOTS, up, g_recv, r)
        spread(-r if r < 4 else 4, piece, piece)
        if r < 4:
            recv["d", r].wait_recv()
            piece = lib_ref.at[at(px, pz + r)]
            if r < 3:
                recv["d", r + 1] = pass_on(piece, piece, SLOTS, down, g_recv, 4 + r)
            spread(r, piece, piece)

    def x_step(dz):
        index = dz + 3
        recv["r", dz].wait_recv()
        piece = lib_ref.at[at(px - 1, pz + dz), first]
        recv["rr", dz] = pass_on(piece, piece, SLOTS // 2, right, g_recv, 23 + index)
        recv["l", dz].wait_recv()
        piece = lib_ref.at[at(px + 1, pz + dz), second]
        recv["ll", dz] = pass_on(piece, piece, SLOTS // 2, left, g_recv, 31 + index)

    def convolve(z):
        wait_all(cols.at[z, pl.ds(0, NP - 1)], a_recv.at[z])

        def step(m, carry):
            rows = pl.ds(m * 128, 128)
            x = cols[z].reshape(size, QW)
            main = dot(bm[0, rows], x) + dot(bm[1, rows], x)
            before = dot(bm[2, rows], x[:, 128:]) + dot(bm[3, rows], x[:, 128:])
            after = dot(bm[4, rows], x[:, :128]) + dot(bm[5, rows], x[:, :128])
            high, low = split2(jnp.concatenate([before, main, after], axis=1))
            out = dot(high, tx[0]) + dot(low, tx[0]) + dot(high, tx[1])
            back[z, pl.ds(m * 8, 8)] = out.astype(BF16).reshape(8, ROWS, QW)
            return carry

        lax.fori_loop(0, size // 128, step, 0)

        def send(i, carry):
            peer = lax.rem(p + i, NP)
            pltpu.make_async_remote_copy(
                back.at[z, peer],
                mixed_ref.at[z, p],
                b_send.at[z],
                b_recv.at[z],
                device_id={"plane": peer},
                device_id_type=MESH,
            ).start()
            return carry

        lax.fori_loop(1, NP, send, 0)
        own_back = pltpu.make_async_copy(back.at[z, p], mixed_ref.at[z, p], b_own.at[z])
        own_back.start()
        return own_back

    owns = []
    z_step(1)
    owns.append(convolve(0))
    x_step(0)
    z_step(2)
    x_step(-1)
    x_step(1)
    owns.append(convolve(1))
    z_step(3)
    x_step(-2)
    x_step(2)
    owns.append(convolve(2))
    z_step(4)
    x_step(-3)
    x_step(3)
    x_step(4)

    for dz in range(-3, 5):
        recv["rr", dz].wait_recv()
        recv["ll", dz].wait_recv()
    for copy in sends:
        copy.wait_send()
    own_copy.wait()
    wait_all(pieces.at[pl.ds(0, (NS - 1) * HELD)], y_send)
    for z in range(ZD):
        wait_all(chunks.at[z, pl.ds(0, NP - 1)], a_send.at[z])
        wait_all(back.at[z, pl.ds(0, NP - 1)], b_send.at[z])
        pltpu.make_async_copy(
            mixed_ref.at[z, pl.ds(0, NP - 1)], mixed_ref.at[z, pl.ds(0, NP - 1)], b_recv.at[z]
        ).wait()
        owns[z].wait()


def exchange(features, x_taps, y_taps, footprint, atlas_tiles):
    size = NP * ROWS
    anywhere = pl.BlockSpec(memory_space=pl.ANY)
    scalars = pl.BlockSpec(memory_space=pltpu.SMEM)
    dma = pltpu.SemaphoreType.DMA
    return pl.pallas_call(
        exchange_kernel,
        out_shape=(
            jax.ShapeDtypeStruct((ZD, NP, ROWS, QW), BF16),
            jax.ShapeDtypeStruct((NP, SLOTS, 16, 128), BF16),
        ),
        in_specs=[anywhere, scalars, scalars, scalars, anywhere],
        out_specs=(anywhere, anywhere),
        scratch_shapes=[
            pltpu.VMEM((ZD, NP, YR, XQ * QW), F32),
            pltpu.VMEM((ZD, NP, ROWS, QW), BF16),
            pltpu.VMEM((ZD, NP, ROWS, QW), BF16),
            pltpu.VMEM((ZD, NP, ROWS, QW), BF16),
            pltpu.VMEM((NS * HELD, 16, 128), BF16),
            pltpu.VMEM((SLOTS, 16, 128), BF16),
            pltpu.VMEM((6, size, size), BF16),
            pltpu.VMEM((2, 2 * QW, QW), BF16),
            dma((ZD + 1,)),
            dma((ZD,)),
            dma((ZD,)),
            dma((ZD,)),
            dma((ZD,)),
            dma((ZD,)),
            dma(()),
            dma(()),
            dma(()),
            dma((39,)),
            dma((39,)),
        ],
        compiler_params=pltpu.CompilerParams(
            collective_id=0, has_side_effects=True, vmem_limit_bytes=40 * 1024 * 1024
        ),
        cost_estimate=pl.CostEstimate(flops=6_000_000_000, bytes_accessed=10_000_000, transcendentals=0),
    )(features, x_taps, y_taps, footprint, atlas_tiles)


def gelu(a):
    inner = a * (0.7978845608028654 + (0.7978845608028654 * 0.044715) * (a * a))
    half = 0.5 * a
    return half + half * jnp.tanh(inner)


def combine_kernel(
    slot_ref,
    base_ref,
    feat_ref,
    mixed_ref,
    lib_ref,
    disp_ref,
    expand_ref,
    bias_ref,
    project_ref,
    out_ref,
    em,
    bias,
    wzy,
    rows_out,
):
    z = pl.program_id(0)
    hid = expand_ref.shape[0]

    @pl.when(z == 0)
    def _():
        lane = lax.broadcasted_iota(jnp.int32, expand_ref.shape, 1) & (ROWS - 1)

        def mask(r, carry):
            em[r] = jnp.where(lane == r, expand_ref[...].astype(F32), 0.0).astype(BF16)
            return carry

        lax.fori_loop(0, ROWS, mask, 0)
        bias[...] = jnp.broadcast_to(bias_ref[...], (hid, QW))

    def tent(place, cells):
        grid = lax.broadcasted_iota(jnp.int32, (cells, BLK), 0).astype(F32)
        return jnp.maximum(0.0, 1.0 - jnp.abs(place - grid))

    def block(n, carry):
        y = n // 2
        xh = lax.rem(n, 2)
        lanes = pl.ds(pl.multiple_of(xh * BLK, BLK), BLK)

        def place(axis, cells):
            base = base_ref[axis, z, y, xh].astype(F32)
            return jnp.clip(disp_ref[axis, 0, pl.ds(y, 1), lanes] + base, 0.0, cells - 1.0)

        wz = tent(place(0, TZ), TZ)
        wy = tent(place(1, TY), TY)
        wx = tent(place(2, TX), TX)
        for i in range(TZ):
            wzy[i * TY : (i + 1) * TY] = wz[i : i + 1] * wy
        slot = slot_ref[z, y, xh]
        total = jnp.zeros((NP, BLK), F32)
        for i in range(TZ):
            interp = jnp.concatenate(
                [(wzy[i * TY + j : i * TY + j + 1] * wx).astype(BF16) for j in range(TY)], axis=0
            )
            tile = jnp.concatenate(
                [
                    jnp.concatenate([lib_ref[16 * h + 2 * i + k, slot] for k in range(2)], axis=1)
                    for h in range(2)
                ],
                axis=0,
            )
            total = total + dot(tile, interp)
        parts = []
        for k in range(2):
            hidden = dot(em[xh * 8 + k * 4 + y], mixed_ref[0]) + bias[...]
            parts.append(dot(project_ref[...], gelu(hidden).astype(BF16)))
        total = total + jnp.concatenate(parts, axis=1)
        for k in range(BLK // 128):
            rows_out[xh * 4 + k, pl.ds(y, NP, stride=YR)] = total[:, k * 128 : (k + 1) * 128]
        return carry

    lax.fori_loop(0, YR * 2, block, 0)

    def write(g, carry):
        rows = pl.ds(pl.multiple_of(g * 8, 8), 8)
        two = jnp.concatenate([rows_out[k, rows] for k in range(8)], axis=1)
        out_ref[pl.ds(g * 2, 2), 0] = feat_ref[pl.ds(g * 2, 2), 0] + two.reshape(2, YR, XQ * QW)
        return carry

    lax.fori_loop(0, NP // 2, write, 0)


def combine(features, mixed, library, block_slot, tile_base, displacement, expand, expand_bias, project):
    hid = expand.shape[0]
    spread = jnp.repeat(expand, ROWS, axis=1)
    scalars = pl.BlockSpec(memory_space=pltpu.SMEM)
    whole = lambda *shape: pl.BlockSpec(shape, lambda z: (0,) * len(shape))
    return pl.pallas_call(
        combine_kernel,
        grid=(ZD,),
        out_shape=jax.ShapeDtypeStruct(features.shape, F32),
        in_specs=[
            scalars,
            scalars,
            pl.BlockSpec((NP, 1, YR, XQ * QW), lambda z: (0, z, 0, 0)),
            pl.BlockSpec((1, NP * ROWS, QW), lambda z: (z, 0, 0)),
            whole(NP, SLOTS, 16, 128),
            pl.BlockSpec((3, 1, YR, XQ * QW), lambda z: (0, z, 0, 0)),
            whole(hid, NP * ROWS),
            whole(hid, 1),
            whole(NP, hid),
        ],
        out_specs=pl.BlockSpec((NP, 1, YR, XQ * QW), lambda z: (0, z, 0, 0)),
        scratch_shapes=[
            pltpu.VMEM((ROWS, hid, NP * ROWS), BF16),
            pltpu.VMEM((hid, QW), F32),
            pltpu.VMEM((TZ * TY, BLK), F32),
            pltpu.VMEM((8, NP * YR, 128), F32),
        ],
        compiler_params=pltpu.CompilerParams(vmem_limit_bytes=40 * 1024 * 1024),
        cost_estimate=pl.CostEstimate(
            flops=4_000_000_000, bytes_accessed=10_000_000, transcendentals=1_600_000
        ),
    )(
        block_slot,
        tile_base,
        features,
        mixed.reshape(ZD, NP * ROWS, QW),
        library,
        displacement,
        spread,
        expand_bias.reshape(hid, 1),
        project,
    )


def body(
    features,
    x_taps,
    y_taps,
    expand,
    expand_bias,
    project,
    atlas_tiles,
    footprint,
    block_slot,
    tile_base,
    displacement,
):
    mixed, library = exchange(features, x_taps, y_taps, footprint, atlas_tiles)
    return combine(
        features, mixed, library, block_slot, tile_base, displacement, expand, expand_bias, project
    )


def solution(mesh):
    return jax.shard_map(
        body,
        mesh=mesh,
        in_specs=(
            P(None, "slab", "plane", None),
            P(),
            P(),
            P(),
            P(),
            P(),
            P("slab", None, None),
            P("slab", None),
            P("slab", "plane", None),
            P(None, "slab", "plane", None),
            P(None, "slab", "plane", None),
        ),
        out_specs=P(None, "slab", "plane", None),
        check_vma=False,
    )
```

time: 415 us -> 113 us (0.27)
  waiting for transfers between devices: 123 us -> 0 us
  Pallas kernels: 0 us -> 105 us
  local copies, waits for them, and re-layouts: 99.2 us -> 7.93 us
  other arithmetic: 56.6 us -> 0 us
  matrix products: 52 us -> 0 us
  loops' own time: 40.5 us -> 0 us
  starting transfers between devices: 40.3 us -> 0 us
    all_to_all x4 -> x0, waiting for transfers between devices: 123 us -> none  [the longest x1 75.4 us: body(): lax.all_to_all(picked.reshape(slab_count, capacity, channels, tile_cells)...]
    pallas_call x0 -> x2, Pallas kernels: none -> 105 us  [the longest x1 82.3 us: exchange(): pl.pallas_call(exchange_kernel, out_shape=(jax.ShapeDtypeStruct((ZD, NP,...]
    dot_general x26 -> x0, matrix products: 52 us -> none  [the longest x24 48.1 us: sample(): return jnp.dot(tile, interp, preferred_element_type=jnp.float32)]
    another operation x1 -> x0, loops' own time: 40.5 us -> none  [body(): sampled = lax.map(sample, (slots, positions))]
    all_to_all x4 -> x0, starting transfers between devices: 40.3 us -> none  [the longest x1 13.8 us: body(): lax.all_to_all(xconv, 'plane', split_axis=3, concat_axis=2, tiled=True)]
    unnamed x31 -> x16, local copies, waits for them, and re-layouts: 39.7 us -> 6.34 us
    convert_element_type x26 -> x0, other arithmetic: 32.6 us -> none  [the longest x24 16.6 us: sample(): interp = (weight_z[:, None, None, :] * weight_y[None, :, None, :] * weigh...]
    all_to_all x5 -> x0, local copies, waits for them, and re-layouts: 17.9 us -> none  [the longest x3 13.4 us: body(): lax.all_to_all(xconv, 'plane', split_axis=3, concat_axis=2, tiled=True)]
  transfers between devices with their start and end apart: 4 -> 0, of which waited for: 3 -> 0; matrix products, arithmetic and copies ran while one was open for 21% -> 0% of each run, Pallas kernels for 0% -> 0%
where the time goes in v1:
time: 113 us
  Pallas kernels  105 us (93%)
  local copies, waits for them, and re-layouts  7.93 us (7%)
    pallas_call x1, Pallas kernels, exchange(): pl.pallas_call(exchange_kernel, out_shape=(jax.ShapeDtypeStruct((ZD, NP,...  82.3 us
    pallas_call x1, Pallas kernels, combine(): pl.pallas_call(combine_kernel, grid=(ZD,), out_shape=jax.ShapeDtypeStruct...  22.4 us
    unnamed x16, local copies, waits for them, and re-layouts  6.34 us

profile of v1, /device:TPU:1, one launch (start us, length us, event | category | flops | bytes accessed | tf_op | source)
XLA Modules:
  0.0 112.7 jit_solution(11375748338971778148)
XLA Ops:
  0.0 0.8 copy.16.slot_ref
  0.8 0.8 copy.17.base_ref
  1.6 0.8 copy.19.bias_ref
  2.4 0.7 broadcast_in_dim.3
  3.1 0.1 copy.18.expand_ref
  3.2 0.0 copy-start
  3.2 1.4 %copy-done = f32[32,3,4,1024]{3,2,1,0:T(4,128)S(1)} copy-done((f32[32,3,4,1024]{3,2,1,0:T(4,128)S(1)}, f32[32,3,4,1024]{3,2,1,0:T(4,128)}, u32[]{:S(2)}) %copy-start) | copy-done | bytes 1572888
  4.6 0.0 copy-start.1
  4.6 1.2 %copy-done.1 = bf16[8,32,2048]{2,1,0:T(8,128)(2,1)S(1)} copy-done((bf16[8,32,2048]{2,1,0:T(8,128)(2,1)S(1)}, bf16[8,32,2048]{2,1,0:T(8,128)(2,1)}, u32[]{:S(2)}) %copy-start.1) | copy-done | bytes 1048600
  5.9 0.0 copy-start.3
  5.9 0.7 copy-done.3
  6.6 0.0 copy-start.4
  6.6 0.7 copy-done.4
  7.3 0.0 copy-start.6
  7.3 0.7 copy-done.6
  7.9 0.0 copy-start.2
  7.9 0.0 copy-start.5
  8.0 82.3 %shard_map.109 = (bf16[3,32,16,256]{3,2,1,0:T(8,128)(2,1)S(1)}, bf16[32,32,16,128]{3,2,1,0:T(8,128)(2,1)S(1)}) custom-call(f32[32,3,4,1024]{3,2,1,0:T(4,128)S(1)} %copy-done, f32[32,31]{1,0:T(8,128)S(1)} %copy-done.3, f32[32,31]{1,0:T(8,128)S(1)} %copy-done.4, s32[1,32]{1,0:T(1,128)S(1)} %copy-done.6, bf16[8,32,2048]{2,1,0:T(8,128)(2,1)S(1)} %copy-done.1), custom_call_target="tpu_custom_call" | custom-call | flops 6000000000 | bytes 10000000 | tf_op jit(solution)/shard_map/pallas_call | solution.py:324
  90.3 0.0 copy-done.2
  90.3 0.0 copy-done.5
  90.3 22.4 %shard_map.110 = f32[32,3,4,1024]{3,2,1,0:T(4,128)} custom-call(s32[3,4,2]{2,1,0:T(4,128)S(1)} %copy.16.slot_ref, s32[3,3,4,2]{3,2,1,0:T(4,128)S(1)} %copy.17.base_ref, f32[32,3,4,1024]{3,2,1,0:T(4,128)S(1)} %copy-done, bf16[3,512,256]{2,1,0:T(8,128)(2,1)S(1)} %bitcast.3, bf16[32,32,16,128]{3,2,1,0:T(8,128)(2,1)S(1)} %get-tuple-element.8.lib_ref, ...), custom_call_target="tpu_custom_call" | custom-call | flops 4000000000 | bytes 10000000 | tf_op jit(solution)/shard_map/pallas_call | solution.py:453
Async XLA Ops:
  3.2 1.4 %copy-start = (f32[32,3,4,1024]{3,2,1,0:T(4,128)S(1)}, f32[32,3,4,1024]{3,2,1,0:T(4,128)}, u32[]{:S(2)}) copy-start(f32[32,3,4,1024]{3,2,1,0:T(4,128)} %feat_ref.3) | copy-start | bytes 4718596
  4.6 1.2 %copy-start.1 = (bf16[8,32,2048]{2,1,0:T(8,128)(2,1)S(1)}, bf16[8,32,2048]{2,1,0:T(8,128)(2,1)}, u32[]{:S(2)}) copy-start(bf16[8,32,2048]{2,1,0:T(8,128)(2,1)} %atlas_ref.1) | copy-start | bytes 3145732
  5.9 0.7 copy-start.3
  6.6 0.7 copy-start.4
  7.3 0.7 copy-start.6
  7.9 82.4 %copy-start.2 = (f32[3,3,4,1024]{3,2,1,0:T(4,128)S(1)}, f32[3,3,4,1024]{3,2,1,0:T(4,128)}, u32[]{:S(2)}) copy-start(f32[3,3,4,1024]{3,2,1,0:T(4,128)} %disp_ref.1) | copy-start | bytes 442372
  7.9 82.4 %copy-start.5 = (bf16[32,128]{1,0:T(8,128)(2,1)S(1)}, bf16[32,128]{1,0:T(8,128)(2,1)}, u32[]{:S(2)}) copy-start(bf16[32,128]{1,0:T(8,128)(2,1)} %project_ref.1) | copy-start | bytes 24580

commit v2 on v1

v2 whole, which is shorter than its diff:
```python
import functools

import jax
import jax.numpy as jnp
from jax import lax
from jax.experimental import pallas as pl
from jax.experimental.pallas import tpu as pltpu
from jax.sharding import PartitionSpec as P

TZ = 8
TY = 16
TX = 16
BLK = 512
KZ = 8
KX = 4
NP = KX * KZ
NS = 16
CAP = 2
SLOTS = NS * CAP
HELD = 8
ZD = 3
YR = 4
XQ = 4
QW = 256
ROWS = XQ * YR
NB = ZD * YR * 2
GROUPS = tuple(range(-3, 5))
F32 = jnp.float32
BF16 = jnp.bfloat16
MESH = pl.DeviceIdType.MESH


def dot(a, b):
    return jnp.dot(a, b, preferred_element_type=F32)


def split2(value):
    high = value.astype(BF16)
    return high, (value - high.astype(F32)).astype(BF16)


def gelu(a):
    inner = a * (0.7978845608028654 + (0.7978845608028654 * 0.044715) * (a * a))
    half = 0.5 * a
    return half + half * jnp.tanh(inner)


def wait_all(ref, sem):
    pltpu.make_async_copy(ref, ref, sem).wait()


def block_kernel(
    feat_ref,
    xt_ref,
    yt_ref,
    expand_ref,
    bias_ref,
    project_ref,
    atlas_ref,
    fp_ref,
    slot_ref,
    base_ref,
    disp_ref,
    out_ref,
    feat,
    chunks,
    cols,
    back,
    mixed,
    pieces,
    picked,
    lib,
    bm,
    tx,
    expand,
    bias,
    wx_all,
    wy_all,
    pz_all,
    wzy,
    acc,
    wide,
    rows_out,
    in_sem,
    a_send,
    a_recv,
    b_send,
    b_recv,
    b_own,
    y_send,
    y_recv,
    g_own,
    g_send,
    g_recv,
):
    s = lax.axis_index("slab")
    p = lax.axis_index("plane")
    px = p // KZ
    pz = lax.rem(p, KZ)
    hid = project_ref.shape[1]
    size = NP * ROWS
    lib = dict(zip(GROUPS, lib))

    barrier = pltpu.get_barrier_semaphore()

    def greet_plane(i, carry):
        pl.semaphore_signal(
            barrier, inc=1, device_id={"plane": lax.rem(p + i, NP)}, device_id_type=MESH
        )
        return carry

    def greet_slab(i, carry):
        pl.semaphore_signal(
            barrier, inc=1, device_id={"slab": lax.rem(s + i, NS)}, device_id_type=MESH
        )
        return carry

    lax.fori_loop(1, NP, greet_plane, 0)
    lax.fori_loop(1, NS, greet_slab, 0)

    loads = [
        pltpu.make_async_copy(feat_ref.at[:, z], feat.at[z], in_sem.at[z]) for z in range(ZD)
    ]
    half = px // 2
    cell = 2 * pz + lax.rem(px, 2)
    atlas_load = pltpu.make_async_copy(
        atlas_ref.at[
            :,
            pl.ds(pl.multiple_of(half * 16, 16), 16),
            pl.ds(pl.multiple_of(cell * 128, 128), 128),
        ],
        pieces.at[pl.ds(s * HELD, HELD)],
        in_sem.at[ZD],
    )
    atlas_load.start()
    for load in loads:
        load.start()

    def make_chunks(z):
        loads[z].wait()

        def step(c, carry):
            block = feat[z, c]
            stacked = jnp.concatenate(
                [block[:, q * QW : (q + 1) * QW] for q in range(XQ)], axis=0
            )
            chunks[z, c] = stacked.astype(BF16)
            return carry

        lax.fori_loop(0, NP, step, 0)

    def send_chunks(z):
        def step(i, carry):
            peer = lax.rem(p + i, NP)
            pltpu.make_async_remote_copy(
                chunks.at[z, peer],
                cols.at[z, p],
                a_send.at[z],
                a_recv.at[z],
                device_id={"plane": peer},
                device_id_type=MESH,
            ).start()
            return carry

        lax.fori_loop(1, NP, step, 0)

    for z in range(ZD):
        make_chunks(z)
        cols[z, p] = chunks[z, p]
    atlas_load.wait()
    pl.semaphore_wait(barrier, NP - 1 + NS - 1)

    def send_piece(i, carry):
        peer = lax.rem(s + i, NS)
        pltpu.make_async_remote_copy(
            pieces.at[pl.ds(s * HELD, HELD)],
            pieces.at[pl.ds(s * HELD, HELD)],
            y_send,
            y_recv,
            device_id={"slab": peer},
            device_id_type=MESH,
        ).start()
        return carry

    lax.fori_loop(1, NS, send_piece, 0)
    for z in range(ZD):
        send_chunks(z)

    def taps_at(index, ref):
        total = jnp.zeros(index.shape, F32)
        for t in range(31):
            total = jnp.where(index == t, ref[p, t], total)
        return total

    def build_rows(m, carry):
        out = lax.broadcasted_iota(jnp.int32, (64, size), 0) + m * 64
        inp = lax.broadcasted_iota(jnp.int32, (64, size), 1)
        row = lambda r: lax.shift_right_logical(r, 4) * 4 + (r & 3)
        quarter = lambda r: lax.shift_right_logical(r, 2) & 3
        weights = taps_at(row(inp) - row(out) + 15, yt_ref)
        for n, shift in enumerate((0, -1, 1)):
            kept = jnp.where(quarter(inp) == quarter(out) + shift, weights, 0.0)
            high, low = split2(kept)
            bm[2 * n, pl.ds(m * 64, 64)] = high
            bm[2 * n + 1, pl.ds(m * 64, 64)] = low
        return carry

    lax.fori_loop(0, size // 64, build_rows, 0)

    def build_x(m, carry):
        k = lax.broadcasted_iota(jnp.int32, (64, QW), 0) + m * 64
        n = lax.broadcasted_iota(jnp.int32, (64, QW), 1)
        high, low = split2(taps_at(k - 128 - n + 15, xt_ref))
        tx[0, pl.ds(m * 64, 64)] = high
        tx[1, pl.ds(m * 64, 64)] = low
        return carry

    lax.fori_loop(0, 8, build_x, 0)

    expand[...] = jnp.transpose(expand_ref[...].astype(F32)).astype(BF16)
    bias[...] = jnp.transpose(jnp.broadcast_to(bias_ref[...], (hid, hid)))

    def tents(n, carry):
        z = n // 8
        y = lax.rem(n, 8) // 2
        xh = lax.rem(n, 2)
        lanes = pl.ds(pl.multiple_of(xh * BLK, BLK), BLK)

        def place(axis, cells):
            base = base_ref[axis, z, xh, y].astype(F32)
            return jnp.clip(disp_ref[axis, z, pl.ds(y, 1), lanes] + base, 0.0, cells - 1.0)

        def tent(axis, cells):
            grid = lax.broadcasted_iota(jnp.int32, (cells, BLK), 0).astype(F32)
            return jnp.maximum(0.0, 1.0 - jnp.abs(place(axis, cells) - grid))

        wy_all[n] = tent(1, TY)
        wx_all[n] = tent(2, TX)
        pz_all[n] = jnp.broadcast_to(place(0, TZ), (8, BLK))
        acc[n] = jnp.zeros((NP, BLK), F32)
        return carry

    lax.fori_loop(0, NB, tents, 0)

    sends = []

    def pass_on(source, target, device, index):
        copy = pltpu.make_async_remote_copy(
            source,
            target,
            g_send.at[len(sends)],
            g_recv.at[index],
            device_id={"plane": device},
            device_id_type=MESH,
        )
        copy.start()
        sends.append(copy)
        return copy

    at = lambda x, z: lax.rem(x + KX, KX) * KZ + lax.rem(z + KZ, KZ)
    column = lambda d: lax.rem(px + d + KX, KX)
    up, down = at(px, pz + 1), at(px, pz - 1)
    right, left = at(px + 1, pz), at(px - 1, pz)
    first, second = pl.ds(0, SLOTS // 2), pl.ds(SLOTS // 2, SLOTS // 2)
    recv = {}

    def spread(dz, source):
        target = lib[dz].at[px]
        recv["r", dz] = pass_on(source, target, right, 7 + dz + 3)
        recv["l", dz] = pass_on(source, target, left, 15 + dz + 3)

    def start_ring():
        wait_all(pieces.at[pl.ds(0, (NS - 1) * HELD)], y_recv)

        def pick(slot, carry):
            tile = jnp.maximum(fp_ref[0, slot], 0)
            picked[slot] = pieces[tile]
            return carry

        lax.fori_loop(0, SLOTS, pick, 0)
        recv["u", 1] = pass_on(picked, lib[-1].at[px], up, 0)
        recv["d", 1] = pass_on(picked, lib[1].at[px], down, 4)
        spread(0, picked)
        copy = pltpu.make_async_copy(picked, lib[0].at[px], g_own)
        copy.start()
        return copy

    def z_step(r):
        recv["u", r].wait_recv()
        dz = -r if r < 4 else 4
        piece = lib[dz].at[px]
        if r < 4:
            recv["u", r + 1] = pass_on(piece, lib[-r - 1 if r < 3 else 4].at[px], up, r)
        spread(dz, piece)
        if r < 4:
            recv["d", r].wait_recv()
            piece = lib[r].at[px]
            if r < 3:
                recv["d", r + 1] = pass_on(piece, lib[r + 1].at[px], down, 4 + r)
            spread(r, piece)

    def x_step(dz):
        recv["r", dz].wait_recv()
        piece = lib[dz].at[column(-1), first]
        recv["rr", dz] = pass_on(piece, piece, right, 23 + dz + 3)
        recv["l", dz].wait_recv()
        piece = lib[dz].at[column(1), second]
        recv["ll", dz] = pass_on(piece, piece, left, 31 + dz + 3)

    def sample(dz):
        recv["rr", dz].wait_recv()
        recv["ll", dz].wait_recv()
        index = lax.rem(pz + dz + KZ, KZ).astype(F32)

        def step(n, carry):
            slot = slot_ref[n // 8, lax.rem(n, 2), lax.rem(n, 8) // 2]
            wz = jnp.maximum(0.0, 1.0 - jnp.abs(pz_all[n] - index))
            wy = wy_all[n]
            wzy[0:8] = wz * wy[0:8]
            wzy[8:16] = wz * wy[8:16]
            wx = wx_all[n]
            interp = jnp.concatenate(
                [(wzy[j : j + 1] * wx).astype(BF16) for j in range(TY)], axis=0
            )
            tile = jnp.concatenate(
                [
                    jnp.concatenate([lib[dz][2 * h + k, slot] for k in range(2)], axis=1)
                    for h in range(2)
                ],
                axis=0,
            )
            acc[n] = acc[n] + dot(tile, interp)
            return carry

        lax.fori_loop(0, NB, step, 0)

    def convolve(z):
        wait_all(cols.at[z, pl.ds(0, NP - 1)], a_recv.at[z])

        def step(m, carry):
            rows = pl.ds(m * 256, 256)
            x = cols[z].reshape(size, QW)
            main = dot(bm[0, rows], x) + dot(bm[1, rows], x)
            before = dot(bm[2, rows], x[:, 128:]) + dot(bm[3, rows], x[:, 128:])
            after = dot(bm[4, rows], x[:, :128]) + dot(bm[5, rows], x[:, :128])
            high, low = split2(jnp.concatenate([before, main, after], axis=1))
            out = dot(high, tx[0]) + dot(low, tx[0]) + dot(high, tx[1])
            back[z, pl.ds(m * 16, 16)] = out.astype(BF16).reshape(16, ROWS, QW)
            return carry

        lax.fori_loop(0, size // 256, step, 0)

        def send(i, carry):
            peer = lax.rem(p + i, NP)
            pltpu.make_async_remote_copy(
                back.at[z, peer],
                mixed.at[z, p],
                b_send.at[z],
                b_recv.at[z],
                device_id={"plane": peer},
                device_id_type=MESH,
            ).start()
            return carry

        lax.fori_loop(1, NP, send, 0)
        own = pltpu.make_async_copy(back.at[z, p], mixed.at[z, p], b_own.at[z])
        own.start()
        return own

    def perceive(z, own):
        wait_all(mixed.at[z, pl.ds(0, NP - 1)], b_recv.at[z])
        own.wait()

        def widen(i, carry):
            two = mixed[z, pl.ds(i * 2, 2)].reshape(2 * ROWS, QW).astype(F32)
            for k in range(2):
                wide[k, pl.ds(pl.multiple_of(i * 32, 32), 32)] = two[:, k * 128 : (k + 1) * 128]
            return carry

        lax.fori_loop(0, NP // 2, widen, 0)

        def step(n, carry):
            y = n // 2
            xh = lax.rem(n, 2)
            x = jnp.concatenate(
                [
                    wide[l, pl.ds(8 * xh + 4 * k + y, NP, stride=ROWS)]
                    for k in range(2)
                    for l in range(2)
                ],
                axis=1,
            ).astype(BF16)
            b = bias[...]
            hidden = dot(expand[...], x) + jnp.concatenate([b] * 4, axis=1)
            acc[z * 8 + n] = acc[z * 8 + n] + dot(project_ref[...], gelu(hidden).astype(BF16))
            return carry

        lax.fori_loop(0, 8, step, 0)

    owns = [convolve(0)]
    own_copy = start_ring()
    owns.append(convolve(1))
    z_step(1)
    owns.append(convolve(2))
    x_step(0)
    z_step(2)
    x_step(-1)
    x_step(1)
    own_copy.wait()
    sample(0)
    z_step(3)
    x_step(-2)
    x_step(2)
    sample(-1)
    z_step(4)
    sample(1)
    x_step(-3)
    x_step(3)
    sample(-2)
    perceive(0, owns[0])
    x_step(4)
    sample(2)
    perceive(1, owns[1])
    sample(-3)
    sample(3)
    perceive(2, owns[2])
    sample(4)

    def finish(z, carry):
        def turn(n, carry):
            y = n // 2
            xh = lax.rem(n, 2)
            value = acc[z * 8 + n]
            for k in range(BLK // 128):
                rows_out[xh * 4 + k, pl.ds(y, NP, stride=YR)] = value[:, k * 128 : (k + 1) * 128]
            return carry

        lax.fori_loop(0, 8, turn, 0)

        def write(g, carry):
            rows = pl.ds(pl.multiple_of(g * 8, 8), 8)
            two = jnp.concatenate([rows_out[k, rows] for k in range(8)], axis=1)
            out_ref[pl.ds(g * 2, 2), z] = two.reshape(2, YR, XQ * QW)
            return carry

        lax.fori_loop(0, NP // 2, write, 0)
        return carry

    lax.fori_loop(0, ZD, finish, 0)

    for copy in sends:
        copy.wait_send()
    wait_all(pieces.at[pl.ds(0, (NS - 1) * HELD)], y_send)
    for z in range(ZD):
        wait_all(chunks.at[z, pl.ds(0, NP - 1)], a_send.at[z])
        wait_all(back.at[z, pl.ds(0, NP - 1)], b_send.at[z])


def body(
    features,
    x_taps,
    y_taps,
    expand,
    expand_bias,
    project,
    atlas_tiles,
    footprint,
    block_slot,
    tile_base,
    displacement,
):
    size = NP * ROWS
    hid = expand.shape[0]
    hbm = pl.BlockSpec(memory_space=pltpu.HBM)
    scalars = pl.BlockSpec(memory_space=pltpu.SMEM)
    vmem = pl.BlockSpec(memory_space=pltpu.VMEM)
    dma = pltpu.SemaphoreType.DMA
    added = pl.pallas_call(
        block_kernel,
        out_shape=jax.ShapeDtypeStruct(features.shape, F32),
        in_specs=[
            hbm,
            scalars,
            scalars,
            vmem,
            vmem,
            vmem,
            hbm,
            scalars,
            scalars,
            scalars,
            vmem,
        ],
        out_specs=vmem,
        scratch_shapes=[
            pltpu.VMEM((ZD, NP, YR, XQ * QW), F32),
            pltpu.VMEM((ZD, NP, ROWS, QW), BF16),
            pltpu.VMEM((ZD, NP, ROWS, QW), BF16),
            pltpu.VMEM((ZD, NP, ROWS, QW), BF16),
            pltpu.VMEM((ZD, NP, ROWS, QW), BF16),
            pltpu.VMEM((NS * HELD, 16, 128), BF16),
            pltpu.VMEM((SLOTS, 16, 128), BF16),
            [pltpu.VMEM((KX, SLOTS, 16, 128), BF16) for _ in GROUPS],
            pltpu.VMEM((6, size, size), BF16),
            pltpu.VMEM((2, 2 * QW, QW), BF16),
            pltpu.VMEM((hid, NP), BF16),
            pltpu.VMEM((hid, hid), F32),
            pltpu.VMEM((NB, TX, BLK), F32),
            pltpu.VMEM((NB, TY, BLK), F32),
            pltpu.VMEM((NB, 8, BLK), F32),
            pltpu.VMEM((TY, BLK), F32),
            pltpu.VMEM((NB, NP, BLK), F32),
            pltpu.VMEM((2, size, 128), F32),
            pltpu.VMEM((8, NP * YR, 128), F32),
            dma((ZD + 1,)),
            dma((ZD,)),
            dma((ZD,)),
            dma((ZD,)),
            dma((ZD,)),
            dma((ZD,)),
            dma(()),
            dma(()),
            dma(()),
            dma((39,)),
            dma((39,)),
        ],
        compiler_params=pltpu.CompilerParams(
            collective_id=0, has_side_effects=True, vmem_limit_bytes=48 * 1024 * 1024
        ),
        cost_estimate=pl.CostEstimate(
            flops=10_000_000_000, bytes_accessed=10_000_000, transcendentals=1_600_000
        ),
    )(
        features,
        x_taps,
        y_taps,
        expand.T,
        expand_bias.reshape(1, hid),
        project,
        atlas_tiles,
        footprint,
        jnp.swapaxes(block_slot, 1, 2),
        jnp.swapaxes(tile_base, 2, 3),
        displacement,
    )
    return features + added


def solution(mesh):
    return jax.shard_map(
        body,
        mesh=mesh,
        in_specs=(
            P(None, "slab", "plane", None),
            P(),
            P(),
            P(),
            P(),
            P(),
            P("slab", None, None),
            P("slab", None),
            P("slab", "plane", None),
            P(None, "slab", "plane", None),
            P(None, "slab", "plane", None),
        ),
        out_specs=P(None, "slab", "plane", None),
        check_vma=False,
    )
```

time: 113 us -> 116 us (1.027)
  other arithmetic: 0 us -> 1.8 us
    unnamed x16 -> x22, local copies, waits for them, and re-layouts: 6.34 us -> 9.06 us
    add x0 -> x1, other arithmetic: none -> 1.8 us  [body(): return features + added]
    pallas_call x2 -> x1, Pallas kernels: 105 us -> 105 us  [body(): pl.pallas_call(block_kernel, out_shape=jax.ShapeDtypeStruct(features.shap...]
where the time goes in v2:
time: 116 us; the launch traced here: 115 us
  Pallas kernels  105 us (91%)
  local copies, waits for them, and re-layouts  9.06 us (8%)
  other arithmetic  1.8 us (2%)
    pallas_call x1, Pallas kernels, body(): pl.pallas_call(block_kernel, out_shape=jax.ShapeDtypeStruct(features.shap...  105 us
    unnamed x22, local copies, waits for them, and re-layouts  9.06 us

profile of v2, /device:TPU:1, one launch (start us, length us, event | category | flops | bytes accessed | tf_op | source)
XLA Modules:
  0.0 115.4 jit_solution(17605565363979746935)
XLA Ops:
  0.0 0.0 copy-start
  0.0 1.4 %copy-done = f32[32,3,4,1024]{3,2,1,0:T(4,128)S(1)} copy-done((f32[32,3,4,1024]{3,2,1,0:T(4,128)S(1)}, f32[32,3,4,1024]{3,2,1,0:T(4,128)}, u32[]{:S(2)}) %copy-start) | copy-done | bytes 1572888
  1.4 0.0 copy-start.1
  1.4 1.2 %copy-done.1 = bf16[8,32,2048]{2,1,0:T(8,128)(2,1)S(1)} copy-done((bf16[8,32,2048]{2,1,0:T(8,128)(2,1)S(1)}, bf16[8,32,2048]{2,1,0:T(8,128)(2,1)}, u32[]{:S(2)}) %copy-start.1) | copy-done | bytes 1048600
  2.6 0.0 copy-start.2
  2.6 0.9 copy-done.2
  3.5 0.0 copy-start.3
  3.5 0.7 copy-done.3
  4.3 0.0 copy-start.4
  4.3 0.7 copy-done.4
  5.0 0.0 copy-start.5
  5.0 0.7 copy-done.5
  5.7 0.0 copy-start.6
  5.7 0.7 copy-done.6
  6.4 0.0 copy-start.7
  6.4 0.7 copy-done.7
  7.1 0.0 copy-start.8
  7.1 0.7 copy-done.8
  7.8 0.0 copy-start.9
  7.8 0.7 copy-done.9
  8.4 0.0 copy-start.10
  8.4 0.7 copy-done.10
  9.1 104.5 %shard_map.109 = f32[32,3,4,1024]{3,2,1,0:T(4,128)S(1)} custom-call(f32[32,3,4,1024]{3,2,1,0:T(4,128)S(1)} %copy-done, f32[32,31]{1,0:T(8,128)S(1)} %copy-done.3, f32[32,31]{1,0:T(8,128)S(1)} %copy-done.4, bf16[32,128]{1,0:T(8,128)(2,1)S(1)} %bitcast.5, f32[1,128]{1,0:T(1,128)S(1)} %bitcast.7, bf16[32,128]{1,0:T(8,128)(2,1)S(1)} %copy-done.7, ...), custom_call_target="tpu_custom_call" | custom-call | flops 10000000000 | bytes 10000000 | tf_op jit(solution)/shard_map/pallas_call | solution.py:478
  113.6 1.8 %add.3 = f32[32,3,4,1024]{3,2,1,0:T(4,128)} add(f32[32,3,4,1024]{3,2,1,0:T(4,128)S(1)} %copy-done, f32[32,3,4,1024]{3,2,1,0:T(4,128)S(1)} %shard_map.109) | non-fusion elementwise | flops 393216 | bytes 4718592 | tf_op jit(solution)/shard_map/add | solution.py:546
Async XLA Ops:
  0.0 1.4 %copy-start = (f32[32,3,4,1024]{3,2,1,0:T(4,128)S(1)}, f32[32,3,4,1024]{3,2,1,0:T(4,128)}, u32[]{:S(2)}) copy-start(f32[32,3,4,1024]{3,2,1,0:T(4,128)} %feat_ref.1) | copy-start | bytes 4718596
  1.4 1.2 %copy-start.1 = (bf16[8,32,2048]{2,1,0:T(8,128)(2,1)S(1)}, bf16[8,32,2048]{2,1,0:T(8,128)(2,1)}, u32[]{:S(2)}) copy-start(bf16[8,32,2048]{2,1,0:T(8,128)(2,1)} %atlas_ref.1) | copy-start | bytes 3145732
  2.6 0.9 copy-start.2
  3.5 0.7 copy-start.3
  4.3 0.7 copy-start.4
  5.0 0.7 copy-start.5
  5.7 0.7 copy-start.6
  6.4 0.7 copy-start.7
  7.1 0.7 copy-start.8
  7.8 0.7 copy-start.9
  8.4 0.7 copy-start.10

commit v3 on v2

--- a/solution.py
+++ b/solution.py
@@ -15,6 +15,7 @@
 KX = 4
 NP = KX * KZ
 NS = 16
+KY = NS // 2
 CAP = 2
 SLOTS = NS * CAP
 HELD = 8
@@ -100,6 +101,10 @@
     hid = project_ref.shape[1]
     size = NP * ROWS
     lib = dict(zip(GROUPS, lib))
+    sy = s // 2
+    core = lax.rem(s, 2)
+    chip = lambda d: lax.rem(sy + d + KY, KY) * 2 + core
+    above, below, beside = chip(1), chip(-1), s + 1 - 2 * core
 
     barrier = pltpu.get_barrier_semaphore()
 
@@ -109,14 +114,9 @@
         )
         return carry
 
-    def greet_slab(i, carry):
-        pl.semaphore_signal(
-            barrier, inc=1, device_id={"slab": lax.rem(s + i, NS)}, device_id_type=MESH
-        )
-        return carry
-
     lax.fori_loop(1, NP, greet_plane, 0)
-    lax.fori_loop(1, NS, greet_slab, 0)
+    for device in (above, below, beside):
+        pl.semaphore_signal(barrier, inc=1, device_id={"slab": device}, device_id_type=MESH)
 
     loads = [
         pltpu.make_async_copy(feat_ref.at[:, z], feat.at[z], in_sem.at[z]) for z in range(ZD)
@@ -147,7 +147,7 @@
             chunks[z, c] = stacked.astype(BF16)
             return carry
 
-        lax.fori_loop(0, NP, step, 0)
+        lax.fori_loop(0, NP, step, 0, unroll=4)
 
     def send_chunks(z):
         def step(i, carry):
@@ -167,25 +167,6 @@
     for z in range(ZD):
         make_chunks(z)
         cols[z, p] = chunks[z, p]
-    atlas_load.wait()
-    pl.semaphore_wait(barrier, NP - 1 + NS - 1)
-
-    def send_piece(i, carry):
-        peer = lax.rem(s + i, NS)
-        pltpu.make_async_remote_copy(
-            pieces.at[pl.ds(s * HELD, HELD)],
-            pieces.at[pl.ds(s * HELD, HELD)],
-            y_send,
-            y_recv,
-            device_id={"slab": peer},
-            device_id_type=MESH,
-        ).start()
-        return carry
-
-    lax.fori_loop(1, NS, send_piece, 0)
-    for z in range(ZD):
-        send_chunks(z)
-
     def taps_at(index, ref):
         total = jnp.zeros(index.shape, F32)
         for t in range(31):
@@ -217,10 +198,36 @@
 
     lax.fori_loop(0, 8, build_x, 0)
 
+    atlas_load.wait()
+    pl.semaphore_wait(barrier, NP - 1 + 3)
+
+    slab_sends = []
+
+    def hand_on(owner, device, index):
+        block = pieces.at[pl.ds(owner * HELD, HELD)]
+        copy = pltpu.make_async_remote_copy(
+            block,
+            block,
+            y_send.at[len(slab_sends)],
+            y_recv.at[index],
+            device_id={"slab": device},
+            device_id_type=MESH,
+        )
+        copy.start()
+        slab_sends.append(copy)
+        return copy
+
+    got = {}
+    got["u", 1] = hand_on(s, above, 0)
+    got["d", 1] = hand_on(s, below, 4)
+    got["c", 0] = hand_on(s, beside, 7)
+    for z in range(ZD):
+        send_chunks(z)
+
     expand[...] = jnp.transpose(expand_ref[...].astype(F32)).astype(BF16)
     bias[...] = jnp.transpose(jnp.broadcast_to(bias_ref[...], (hid, hid)))
 
-    def tents(n, carry):
+    def tents_of(n, carry):
         z = n // 8
         y = lax.rem(n, 8) // 2
         xh = lax.rem(n, 2)
@@ -240,7 +247,7 @@
         acc[n] = jnp.zeros((NP, BLK), F32)
         return carry
 
-    lax.fori_loop(0, NB, tents, 0)
+    tents = lambda: lax.fori_loop(0, NB, tents_of, 0)
 
     sends = []
 
@@ -270,7 +277,18 @@
         recv["l", dz] = pass_on(source, target, left, 15 + dz + 3)
 
     def start_ring():
-        wait_all(pieces.at[pl.ds(0, (NS - 1) * HELD)], y_recv)
+        for r in range(1, 5):
+            got["u", r].wait_recv()
+            if r < 4:
+                got["u", r + 1] = hand_on(chip(-r), above, r)
+            got["c", -r] = hand_on(chip(-r), beside, 7 + r)
+            if r < 4:
+                got["d", r].wait_recv()
+                if r < 3:
+                    got["d", r + 1] = hand_on(chip(r), below, 4 + r)
+                got["c", r] = hand_on(chip(r), beside, 11 + r)
+        for r in range(-4, 4):
+            got["c", r].wait_recv()
 
         def pick(slot, carry):
             tile = jnp.maximum(fp_ref[0, slot], 0)
@@ -307,24 +325,32 @@
         piece = lib[dz].at[column(1), second]
         recv["ll", dz] = pass_on(piece, piece, left, 31 + dz + 3)
 
-    def sample(dz):
-        recv["rr", dz].wait_recv()
-        recv["ll", dz].wait_recv()
-        index = lax.rem(pz + dz + KZ, KZ).astype(F32)
+    def sample(*groups):
+        for dz in groups:
+            recv["rr", dz].wait_recv()
+            recv["ll", dz].wait_recv()
+        indices = [lax.rem(pz + dz + KZ, KZ).astype(F32) for dz in groups]
 
         def step(n, carry):
             slot = slot_ref[n // 8, lax.rem(n, 2), lax.rem(n, 8) // 2]
-            wz = jnp.maximum(0.0, 1.0 - jnp.abs(pz_all[n] - index))
-            wy = wy_all[n]
-            wzy[0:8] = wz * wy[0:8]
-            wzy[8:16] = wz * wy[8:16]
-            wx = wx_all[n]
+            wy, wx, place = wy_all[n], wx_all[n], pz_all[n]
+            for g, index in enumerate(indices):
+                wz = jnp.maximum(0.0, 1.0 - jnp.abs(place - index))
+                wzy[g, 0:8] = wz * wy[0:8]
+                wzy[g, 8:16] = wz * wy[8:16]
             interp = jnp.concatenate(
-                [(wzy[j : j + 1] * wx).astype(BF16) for j in range(TY)], axis=0
+                [
+                    (wzy[g, j : j + 1] * wx).astype(BF16)
+                    for g in range(len(groups))
+                    for j in range(TY)
+                ],
+                axis=0,
             )
             tile = jnp.concatenate(
                 [
-                    jnp.concatenate([lib[dz][2 * h + k, slot] for k in range(2)], axis=1)
+                    jnp.concatenate(
+                        [lib[dz][2 * h + k, slot] for dz in groups for k in range(2)], axis=1
+                    )
                     for h in range(2)
                 ],
                 axis=0,
@@ -332,7 +358,7 @@
             acc[n] = acc[n] + dot(tile, interp)
             return carry
 
-        lax.fori_loop(0, NB, step, 0)
+        lax.fori_loop(0, NB, step, 0, unroll=4)
 
     def convolve(z):
         wait_all(cols.at[z, pl.ds(0, NP - 1)], a_recv.at[z])
@@ -377,7 +403,7 @@
                 wide[k, pl.ds(pl.multiple_of(i * 32, 32), 32)] = two[:, k * 128 : (k + 1) * 128]
             return carry
 
-        lax.fori_loop(0, NP // 2, widen, 0)
+        lax.fori_loop(0, NP // 2, widen, 0, unroll=4)
 
         def step(n, carry):
             y = n // 2
@@ -395,35 +421,33 @@
             acc[z * 8 + n] = acc[z * 8 + n] + dot(project_ref[...], gelu(hidden).astype(BF16))
             return carry
 
-        lax.fori_loop(0, 8, step, 0)
-
+        lax.fori_loop(0, 8, step, 0, unroll=2)
+
+    own_copy = start_ring()
+    tents()
     owns = [convolve(0)]
-    own_copy = start_ring()
+    z_step(1)
     owns.append(convolve(1))
-    z_step(1)
-    owns.append(convolve(2))
     x_step(0)
     z_step(2)
+    owns.append(convolve(2))
     x_step(-1)
     x_step(1)
+    z_step(3)
     own_copy.wait()
     sample(0)
-    z_step(3)
+    z_step(4)
     x_step(-2)
     x_step(2)
-    sample(-1)
-    z_step(4)
-    sample(1)
+    sample(-1, 1)
+    perceive(0, owns[0])
     x_step(-3)
     x_step(3)
-    sample(-2)
-    perceive(0, owns[0])
+    sample(-2, 2)
+    perceive(1, owns[1])
     x_step(4)
-    sample(2)
-    perceive(1, owns[1])
-    sample(-3)
-    sample(3)
     perceive(2, owns[2])
+    sample(-3, 3)
     sample(4)
 
     def finish(z, carry):
@@ -450,7 +474,8 @@
 
     for copy in sends:
         copy.wait_send()
-    wait_all(pieces.at[pl.ds(0, (NS - 1) * HELD)], y_send)
+    for copy in slab_sends:
+        copy.wait_send()
     for z in range(ZD):
         wait_all(chunks.at[z, pl.ds(0, NP - 1)], a_send.at[z])
         wait_all(back.at[z, pl.ds(0, NP - 1)], b_send.at[z])
@@ -508,7 +533,7 @@
             pltpu.VMEM((NB, TX, BLK), F32),
             pltpu.VMEM((NB, TY, BLK), F32),
             pltpu.VMEM((NB, 8, BLK), F32),
-            pltpu.VMEM((TY, BLK), F32),
+            pltpu.VMEM((2, TY, BLK), F32),
             pltpu.VMEM((NB, NP, BLK), F32),
             pltpu.VMEM((2, size, 128), F32),
             pltpu.VMEM((8, NP * YR, 128), F32),
@@ -518,14 +543,14 @@
             dma((ZD,)),
             dma((ZD,)),
             dma((ZD,)),
-            dma(()),
-            dma(()),
+            dma((15,)),
+            dma((15,)),
             dma(()),
             dma((39,)),
             dma((39,)),
         ],
         compiler_params=pltpu.CompilerParams(
-            collective_id=0, has_side_effects=True, vmem_limit_bytes=48 * 1024 * 1024
+            collective_id=0, has_side_effects=True, vmem_limit_bytes=60 * 1024 * 1024
         ),
         cost_estimate=pl.CostEstimate(
             flops=10_000_000_000, bytes_accessed=10_000_000, transcendentals=1_600_000

time: 116 us -> 95.6 us (0.82)
  Pallas kernels: 105 us -> 91.9 us
  local copies, waits for them, and re-layouts: 9.06 us -> 0.01 us
  other arithmetic: 1.8 us -> 3.21 us
    pallas_call x1, Pallas kernels: 105 us -> 91.9 us  [body(): pl.pallas_call(block_kernel, out_shape=jax.ShapeDtypeStruct(features.shap...]
    unnamed x22 -> x2, local copies, waits for them, and re-layouts: 9.06 us -> 0.01 us
    add x1, other arithmetic: 1.8 us -> 3.21 us  [body(): return features + added]
where the time goes in v3:
time: 95.6 us; the launch traced here: 95.1 us
  Pallas kernels  91.9 us (96%)
  other arithmetic  3.21 us (3%)
    pallas_call x1, Pallas kernels, body(): pl.pallas_call(block_kernel, out_shape=jax.ShapeDtypeStruct(features.shap...  91.9 us
    add x1, other arithmetic, body(): return features + added  3.21 us

profile of v3, /device:TPU:1, one launch (start us, length us, event | category | flops | bytes accessed | tf_op | source)
XLA Modules:
  0.0 95.1 jit_solution(13835279159400054302)
XLA Ops:
  0.0 0.0 copy-start
  0.0 91.9 %shard_map.109 = f32[32,3,4,1024]{3,2,1,0:T(4,128)} custom-call(f32[32,3,4,1024]{3,2,1,0:T(4,128)} %feat_ref.1, f32[32,31]{1,0:T(8,128)} %xt_ref.1, f32[32,31]{1,0:T(8,128)} %yt_ref.1, bf16[32,128]{1,0:T(8,128)(2,1)} %bitcast.5, f32[1,128]{1,0:T(1,128)} %bitcast.7, bf16[32,128]{1,0:T(8,128)(2,1)} %project_ref.1, bf16[8,32,2048]{2,1,0:T(8,128)(2,1)} %atlas_ref.1, ...), custom_call_target="tpu_custom_call" | custom-call | flops 10000000000 | bytes 10000000 | tf_op jit(solution)/shard_map/pallas_call | solution.py:503
  91.9 0.0 copy-done
  91.9 3.2 %add.3 = f32[32,3,4,1024]{3,2,1,0:T(4,128)} add(f32[32,3,4,1024]{3,2,1,0:T(4,128)S(1)} %copy-done, f32[32,3,4,1024]{3,2,1,0:T(4,128)} %shard_map.109) | non-fusion elementwise | flops 393216 | bytes 4718592 | tf_op jit(solution)/shard_map/add | solution.py:571
Async XLA Ops:
  0.0 91.9 %copy-start = (f32[32,3,4,1024]{3,2,1,0:T(4,128)S(1)}, f32[32,3,4,1024]{3,2,1,0:T(4,128)}, u32[]{:S(2)}) copy-start(f32[32,3,4,1024]{3,2,1,0:T(4,128)} %feat_ref.1) | copy-start | bytes 4718596

commit v4 on v3

--- a/solution.py
+++ b/solution.py
@@ -25,7 +25,9 @@
 QW = 256
 ROWS = XQ * YR
 NB = ZD * YR * 2
-GROUPS = tuple(range(-3, 5))
+RU, RD = 2, 2
+GROUPS = tuple(range(-RU, RD + 1))
+DIRECT = tuple(range(RD + 1, KZ - RU))
 F32 = jnp.float32
 BF16 = jnp.bfloat16
 MESH = pl.DeviceIdType.MESH
@@ -59,6 +61,7 @@
     project_ref,
     atlas_ref,
     fp_ref,
+    row_ref,
     slot_ref,
     base_ref,
     disp_ref,
@@ -71,6 +74,11 @@
     pieces,
     picked,
     lib,
+    straight,
+    held,
+    stage,
+    rows_all,
+    wanted,
     bm,
     tx,
     expand,
@@ -93,6 +101,12 @@
     g_own,
     g_send,
     g_recv,
+    f_send,
+    f_recv,
+    f_local,
+    d_load,
+    d_send,
+    d_recv,
 ):
     s = lax.axis_index("slab")
     p = lax.axis_index("plane")
@@ -101,10 +115,14 @@
     hid = project_ref.shape[1]
     size = NP * ROWS
     lib = dict(zip(GROUPS, lib))
+    straight, held, stage = (dict(zip(DIRECT, refs)) for refs in (straight, held, stage))
     sy = s // 2
     core = lax.rem(s, 2)
     chip = lambda d: lax.rem(sy + d + KY, KY) * 2 + core
-    above, below, beside = chip(1), chip(-1), s + 1 - 2 * core
+    beside = s + 1 - 2 * core
+    mine = pl.ds((core * KY + sy) * HELD, HELD)
+    near = pl.ds(core * KY * HELD, KY * HELD)
+    far = pl.ds((1 - core) * KY * HELD, KY * HELD)
 
     barrier = pltpu.get_barrier_semaphore()
 
@@ -115,8 +133,14 @@
         return carry
 
     lax.fori_loop(1, NP, greet_plane, 0)
-    for device in (above, below, beside):
-        pl.semaphore_signal(barrier, inc=1, device_id={"slab": device}, device_id_type=MESH)
+
+    def greet_slab(i, carry):
+        pl.semaphore_signal(
+            barrier, inc=1, device_id={"slab": lax.rem(s + i, NS)}, device_id_type=MESH
+        )
+        return carry
+
+    lax.fori_loop(1, NS, greet_slab, 0)
 
     loads = [
         pltpu.make_async_copy(feat_ref.at[:, z], feat.at[z], in_sem.at[z]) for z in range(ZD)
@@ -129,11 +153,24 @@
             pl.ds(pl.multiple_of(half * 16, 16), 16),
             pl.ds(pl.multiple_of(cell * 128, 128), 128),
         ],
-        pieces.at[pl.ds(s * HELD, HELD)],
+        pieces.at[mine],
         in_sem.at[ZD],
     )
     atlas_load.start()
-    for load in loads:
+    held_loads = []
+    for n, dz in enumerate(DIRECT):
+        for q in range(KX):
+            start = (2 * lax.rem(pz + dz + KZ, KZ) + q % 2) * 128
+            held_loads.append(
+                pltpu.make_async_copy(
+                    atlas_ref.at[
+                        :, pl.ds(q // 2 * 16, 16), pl.ds(pl.multiple_of(start, 128), 128)
+                    ],
+                    held[dz].at[q],
+                    d_load.at[n * KX + q],
+                )
+            )
+    for load in loads + held_loads:
         load.start()
 
     def make_chunks(z):
@@ -198,32 +235,6 @@
 
     lax.fori_loop(0, 8, build_x, 0)
 
-    atlas_load.wait()
-    pl.semaphore_wait(barrier, NP - 1 + 3)
-
-    slab_sends = []
-
-    def hand_on(owner, device, index):
-        block = pieces.at[pl.ds(owner * HELD, HELD)]
-        copy = pltpu.make_async_remote_copy(
-            block,
-            block,
-            y_send.at[len(slab_sends)],
-            y_recv.at[index],
-            device_id={"slab": device},
-            device_id_type=MESH,
-        )
-        copy.start()
-        slab_sends.append(copy)
-        return copy
-
-    got = {}
-    got["u", 1] = hand_on(s, above, 0)
-    got["d", 1] = hand_on(s, below, 4)
-    got["c", 0] = hand_on(s, beside, 7)
-    for z in range(ZD):
-        send_chunks(z)
-
     expand[...] = jnp.transpose(expand_ref[...].astype(F32)).astype(BF16)
     bias[...] = jnp.transpose(jnp.broadcast_to(bias_ref[...], (hid, hid)))
 
@@ -247,7 +258,39 @@
         acc[n] = jnp.zeros((NP, BLK), F32)
         return carry
 
-    tents = lambda: lax.fori_loop(0, NB, tents_of, 0)
+    lax.fori_loop(0, NB, tents_of, 0)
+
+    atlas_load.wait()
+    pl.semaphore_wait(barrier, NP - 1 + NS - 1)
+
+    def send_row(i, carry):
+        pltpu.make_async_remote_copy(
+            row_ref,
+            rows_all.at[s],
+            f_send,
+            f_recv,
+            device_id={"slab": lax.rem(s + i, NS)},
+            device_id_type=MESH,
+        ).start()
+        return carry
+
+    lax.fori_loop(1, NS, send_row, 0)
+    rows_all[s] = row_ref[...]
+
+    def send_piece(i, carry):
+        pltpu.make_async_remote_copy(
+            pieces.at[mine],
+            pieces.at[mine],
+            y_send.at[0],
+            y_recv.at[0],
+            device_id={"slab": chip(i)},
+            device_id_type=MESH,
+        ).start()
+        return carry
+
+    lax.fori_loop(1, KY, send_piece, 0)
+    for z in range(ZD):
+        send_chunks(z)
 
     sends = []
 
@@ -265,70 +308,89 @@
         return copy
 
     at = lambda x, z: lax.rem(x + KX, KX) * KZ + lax.rem(z + KZ, KZ)
-    column = lambda d: lax.rem(px + d + KX, KX)
-    up, down = at(px, pz + 1), at(px, pz - 1)
-    right, left = at(px + 1, pz), at(px - 1, pz)
-    first, second = pl.ds(0, SLOTS // 2), pl.ds(SLOTS // 2, SLOTS // 2)
     recv = {}
+    around = (("r", 1), ("l", -1), ("o", 2))
 
     def spread(dz, source):
-        target = lib[dz].at[px]
-        recv["r", dz] = pass_on(source, target, right, 7 + dz + 3)
-        recv["l", dz] = pass_on(source, target, left, 15 + dz + 3)
+        for n, (way, dx) in enumerate(around):
+            recv[way, dz] = pass_on(source, lib[dz].at[px], at(px + dx, pz), 7 + 8 * n + dz + 3)
 
     def start_ring():
-        for r in range(1, 5):
-            got["u", r].wait_recv()
-            if r < 4:
-                got["u", r + 1] = hand_on(chip(-r), above, r)
-            got["c", -r] = hand_on(chip(-r), beside, 7 + r)
-            if r < 4:
-                got["d", r].wait_recv()
-                if r < 3:
-                    got["d", r + 1] = hand_on(chip(r), below, 4 + r)
-                got["c", r] = hand_on(chip(r), beside, 11 + r)
-        for r in range(-4, 4):
-            got["c", r].wait_recv()
+        wait_all(pieces.at[pl.ds(0, (KY - 1) * HELD)], y_recv.at[0])
+        pltpu.make_async_remote_copy(
+            pieces.at[near],
+            pieces.at[near],
+            y_send.at[1],
+            y_recv.at[1],
+            device_id={"slab": beside},
+            device_id_type=MESH,
+        ).start()
+        wait_all(pieces.at[far], y_recv.at[1])
 
         def pick(slot, carry):
             tile = jnp.maximum(fp_ref[0, slot], 0)
-            picked[slot] = pieces[tile]
+            owner = tile // HELD
+            place = lax.rem(owner, 2) * KY + owner // 2
+            picked[slot] = pieces[place * HELD + lax.rem(tile, HELD)]
             return carry
 
         lax.fori_loop(0, SLOTS, pick, 0)
-        recv["u", 1] = pass_on(picked, lib[-1].at[px], up, 0)
-        recv["d", 1] = pass_on(picked, lib[1].at[px], down, 4)
         spread(0, picked)
+        for dz in GROUPS:
+            if dz:
+                recv["z", dz] = pass_on(picked, lib[dz].at[px], at(px, pz - dz), dz + 3)
         copy = pltpu.make_async_copy(picked, lib[0].at[px], g_own)
         copy.start()
         return copy
 
-    def z_step(r):
-        recv["u", r].wait_recv()
-        dz = -r if r < 4 else 4
-        piece = lib[dz].at[px]
-        if r < 4:
-            recv["u", r + 1] = pass_on(piece, lib[-r - 1 if r < 3 else 4].at[px], up, r)
-        spread(dz, piece)
-        if r < 4:
-            recv["d", r].wait_recv()
-            piece = lib[r].at[px]
-            if r < 3:
-                recv["d", r + 1] = pass_on(piece, lib[r + 1].at[px], down, 4 + r)
-            spread(r, piece)
-
-    def x_step(dz):
-        recv["r", dz].wait_recv()
-        piece = lib[dz].at[column(-1), first]
-        recv["rr", dz] = pass_on(piece, piece, right, 23 + dz + 3)
-        recv["l", dz].wait_recv()
-        piece = lib[dz].at[column(1), second]
-        recv["ll", dz] = pass_on(piece, piece, left, 31 + dz + 3)
+    def start_direct():
+        wait_all(rows_all.at[pl.ds(0, NS - 1)], f_recv)
+        local = pltpu.make_async_copy(rows_all, wanted, f_local)
+        local.start()
+        for load in held_loads:
+            load.wait()
+        local.wait()
+        for n, dz in enumerate(DIRECT):
+
+            def fill(j, carry):
+                tile = wanted[j // CAP, 0, s * CAP + lax.rem(j, CAP)] - s * HELD
+                tile = jnp.clip(tile, 0, HELD - 1)
+                for q in range(KX):
+                    stage[dz][j, q] = held[dz][q, tile]
+                return carry
+
+            lax.fori_loop(0, SLOTS, fill, 0, unroll=2)
+
+            def send(i, carry):
+                peer = lax.rem(s + i, NS)
+                pltpu.make_async_remote_copy(
+                    stage[dz].at[pl.ds(peer * CAP, CAP)],
+                    straight[dz].at[pl.ds(s * CAP, CAP)],
+                    d_send.at[n],
+                    d_recv.at[n],
+                    device_id={"slab": peer},
+                    device_id_type=MESH,
+                ).start()
+                return carry
+
+            lax.fori_loop(1, NS, send, 0)
+            straight[dz][pl.ds(s * CAP, CAP)] = stage[dz][pl.ds(s * CAP, CAP)]
+
+    def z_step(dz):
+        recv["z", dz].wait_recv()
+        spread(dz, lib[dz].at[px])
 
     def sample(*groups):
         for dz in groups:
-            recv["rr", dz].wait_recv()
-            recv["ll", dz].wait_recv()
+            if dz in GROUPS:
+                for way, _ in around:
+                    recv[way, dz].wait_recv()
+            else:
+                wait_all(straight[dz].at[pl.ds(0, SLOTS - CAP)], d_recv.at[DIRECT.index(dz)])
+
+        def part(dz, q, slot):
+            return lib[dz][q, slot] if dz in GROUPS else straight[dz][slot, q]
+
         indices = [lax.rem(pz + dz + KZ, KZ).astype(F32) for dz in groups]
 
         def step(n, carry):
@@ -349,7 +411,7 @@
             tile = jnp.concatenate(
                 [
                     jnp.concatenate(
-                        [lib[dz][2 * h + k, slot] for dz in groups for k in range(2)], axis=1
+                        [part(dz, 2 * h + k, slot) for dz in groups for k in range(2)], axis=1
                     )
                     for h in range(2)
                 ],
@@ -423,32 +485,25 @@
 
         lax.fori_loop(0, 8, step, 0, unroll=2)
 
+    start_direct()
     own_copy = start_ring()
-    tents()
     owns = [convolve(0)]
     z_step(1)
+    z_step(-1)
+    z_step(2)
+    z_step(-2)
     owns.append(convolve(1))
-    x_step(0)
-    z_step(2)
     owns.append(convolve(2))
-    x_step(-1)
-    x_step(1)
-    z_step(3)
     own_copy.wait()
     sample(0)
-    z_step(4)
-    x_step(-2)
-    x_step(2)
+    sample(3)
+    perceive(0, owns[0])
     sample(-1, 1)
-    perceive(0, owns[0])
-    x_step(-3)
-    x_step(3)
+    perceive(1, owns[1])
+    sample(4)
     sample(-2, 2)
-    perceive(1, owns[1])
-    x_step(4)
     perceive(2, owns[2])
-    sample(-3, 3)
-    sample(4)
+    sample(5)
 
     def finish(z, carry):
         def turn(n, carry):
@@ -474,8 +529,11 @@
 
     for copy in sends:
         copy.wait_send()
-    for copy in slab_sends:
-        copy.wait_send()
+    wait_all(pieces.at[pl.ds(0, (KY - 1) * HELD)], y_send.at[0])
+    wait_all(pieces.at[near], y_send.at[1])
+    wait_all(rows_all.at[pl.ds(0, NS - 1)], f_send)
+    for n, dz in enumerate(DIRECT):
+        wait_all(stage[dz].at[pl.ds(0, SLOTS - CAP)], d_send.at[n])
     for z in range(ZD):
         wait_all(chunks.at[z, pl.ds(0, NP - 1)], a_send.at[z])
         wait_all(back.at[z, pl.ds(0, NP - 1)], b_send.at[z])
@@ -512,6 +570,7 @@
             vmem,
             hbm,
             scalars,
+            vmem,
             scalars,
             scalars,
             vmem,
@@ -526,6 +585,11 @@
             pltpu.VMEM((NS * HELD, 16, 128), BF16),
             pltpu.VMEM((SLOTS, 16, 128), BF16),
             [pltpu.VMEM((KX, SLOTS, 16, 128), BF16) for _ in GROUPS],
+            [pltpu.VMEM((SLOTS, KX, 16, 128), BF16) for _ in DIRECT],
+            [pltpu.VMEM((KX, HELD, 16, 128), BF16) for _ in DIRECT],
+            [pltpu.VMEM((SLOTS, KX, 16, 128), BF16) for _ in DIRECT],
+            pltpu.VMEM((NS, 1, SLOTS), jnp.int32),
+            pltpu.SMEM((NS, 1, SLOTS), jnp.int32),
             pltpu.VMEM((6, size, size), BF16),
             pltpu.VMEM((2, 2 * QW, QW), BF16),
             pltpu.VMEM((hid, NP), BF16),
@@ -543,11 +607,17 @@
             dma((ZD,)),
             dma((ZD,)),
             dma((ZD,)),
-            dma((15,)),
-            dma((15,)),
+            dma((2,)),
+            dma((2,)),
             dma(()),
             dma((39,)),
             dma((39,)),
+            dma(()),
+            dma(()),
+            dma(()),
+            dma((len(DIRECT) * KX,)),
+            dma((len(DIRECT),)),
+            dma((len(DIRECT),)),
         ],
         compiler_params=pltpu.CompilerParams(
             collective_id=0, has_side_effects=True, vmem_limit_bytes=60 * 1024 * 1024
@@ -563,6 +633,7 @@
         expand_bias.reshape(1, hid),
         project,
         atlas_tiles,
+        footprint,
         footprint,
         jnp.swapaxes(block_slot, 1, 2),
         jnp.swapaxes(tile_base, 2, 3),

time: 95.6 us -> 90.3 us (0.945)
  Pallas kernels: 91.9 us -> 86.8 us
    pallas_call x1, Pallas kernels: 91.9 us -> 86.8 us  [body(): pl.pallas_call(block_kernel, out_shape=jax.ShapeDtypeStruct(features.shap...]
where the time goes in v4:
time: 90.3 us; the launch traced here: 90.1 us
  Pallas kernels  86.8 us (96%)
  other arithmetic  3.21 us (4%)
    pallas_call x1, Pallas kernels, body(): pl.pallas_call(block_kernel, out_shape=jax.ShapeDtypeStruct(features.shap...  86.8 us
    add x1, other arithmetic, body(): return features + added  3.21 us

profile of v4, /device:TPU:1, one launch (start us, length us, event | category | flops | bytes accessed | tf_op | source)
XLA Modules:
  0.0 90.1 jit_solution(14327850482588377988)
XLA Ops:
  0.0 0.0 copy-start
  0.0 86.8 %shard_map.109 = f32[32,3,4,1024]{3,2,1,0:T(4,128)} custom-call(f32[32,3,4,1024]{3,2,1,0:T(4,128)} %feat_ref.1, f32[32,31]{1,0:T(8,128)} %xt_ref.1, f32[32,31]{1,0:T(8,128)} %yt_ref.1, bf16[32,128]{1,0:T(8,128)(2,1)} %bitcast.5, f32[1,128]{1,0:T(1,128)} %bitcast.7, bf16[32,128]{1,0:T(8,128)(2,1)} %project_ref.1, bf16[8,32,2048]{2,1,0:T(8,128)(2,1)} %atlas_ref.1, ...), custom_call_target="tpu_custom_call" | custom-call | flops 10000000000 | bytes 10000000 | tf_op jit(solution)/shard_map/pallas_call | solution.py:561
  86.8 0.0 copy-done
  86.8 3.2 %add.3 = f32[32,3,4,1024]{3,2,1,0:T(4,128)} add(f32[32,3,4,1024]{3,2,1,0:T(4,128)S(1)} %copy-done, f32[32,3,4,1024]{3,2,1,0:T(4,128)} %shard_map.109) | non-fusion elementwise | flops 393216 | bytes 4718592 | tf_op jit(solution)/shard_map/add | solution.py:642
Async XLA Ops:
  0.0 86.8 %copy-start = (f32[32,3,4,1024]{3,2,1,0:T(4,128)S(1)}, f32[32,3,4,1024]{3,2,1,0:T(4,128)}, u32[]{:S(2)}) copy-start(f32[32,3,4,1024]{3,2,1,0:T(4,128)} %feat_ref.1) | copy-start | bytes 4718596

commit v5 on v4

--- a/solution.py
+++ b/solution.py
@@ -25,7 +25,7 @@
 QW = 256
 ROWS = XQ * YR
 NB = ZD * YR * 2
-RU, RD = 2, 2
+RU, RD = 1, 2
 GROUPS = tuple(range(-RU, RD + 1))
 DIRECT = tuple(range(RD + 1, KZ - RU))
 F32 = jnp.float32
@@ -315,7 +315,7 @@
         for n, (way, dx) in enumerate(around):
             recv[way, dz] = pass_on(source, lib[dz].at[px], at(px + dx, pz), 7 + 8 * n + dz + 3)
 
-    def start_ring():
+    def hand_over():
         wait_all(pieces.at[pl.ds(0, (KY - 1) * HELD)], y_recv.at[0])
         pltpu.make_async_remote_copy(
             pieces.at[near],
@@ -325,6 +325,8 @@
             device_id={"slab": beside},
             device_id_type=MESH,
         ).start()
+
+    def start_ring():
         wait_all(pieces.at[far], y_recv.at[1])
 
         def pick(slot, carry):
@@ -486,24 +488,25 @@
         lax.fori_loop(0, 8, step, 0, unroll=2)
 
     start_direct()
+    hand_over()
+    owns = [convolve(0)]
     own_copy = start_ring()
-    owns = [convolve(0)]
+    owns.append(convolve(1))
     z_step(1)
     z_step(-1)
+    owns.append(convolve(2))
     z_step(2)
-    z_step(-2)
-    owns.append(convolve(1))
-    owns.append(convolve(2))
     own_copy.wait()
-    sample(0)
     sample(3)
     perceive(0, owns[0])
+    sample(0)
+    sample(4)
+    perceive(1, owns[1])
     sample(-1, 1)
-    perceive(1, owns[1])
-    sample(4)
-    sample(-2, 2)
+    sample(5)
     perceive(2, owns[2])
-    sample(5)
+    sample(2)
+    sample(6)
 
     def finish(z, carry):
         def turn(n, carry):

time: 90.3 us -> 79.7 us (0.88)
  Pallas kernels: 86.8 us -> 76.3 us
    pallas_call x1, Pallas kernels: 86.8 us -> 76.3 us  [body(): pl.pallas_call(block_kernel, out_shape=jax.ShapeDtypeStruct(features.shap...]
where the time goes in v5:
time: 79.7 us; the launch traced here: 79.5 us
  Pallas kernels  76.3 us (96%)
  other arithmetic  3.21 us (4%)
    pallas_call x1, Pallas kernels, body(): pl.pallas_call(block_kernel, out_shape=jax.ShapeDtypeStruct(features.shap...  76.3 us
    add x1, other arithmetic, body(): return features + added  3.21 us

profile of v5, /device:TPU:1, one launch (start us, length us, event | category | flops | bytes accessed | tf_op | source)
XLA Modules:
  0.0 79.5 jit_solution(16352478286223888811)
XLA Ops:
  0.0 0.0 copy-start
  0.0 76.3 %shard_map.109 = f32[32,3,4,1024]{3,2,1,0:T(4,128)} custom-call(f32[32,3,4,1024]{3,2,1,0:T(4,128)} %feat_ref.1, f32[32,31]{1,0:T(8,128)} %xt_ref.1, f32[32,31]{1,0:T(8,128)} %yt_ref.1, bf16[32,128]{1,0:T(8,128)(2,1)} %bitcast.5, f32[1,128]{1,0:T(1,128)} %bitcast.7, bf16[32,128]{1,0:T(8,128)(2,1)} %project_ref.1, bf16[8,32,2048]{2,1,0:T(8,128)(2,1)} %atlas_ref.1, ...), custom_call_target="tpu_custom_call" | custom-call | flops 10000000000 | bytes 10000000 | tf_op jit(solution)/shard_map/pallas_call | solution.py:564
  76.3 0.0 copy-done
  76.3 3.2 %add.3 = f32[32,3,4,1024]{3,2,1,0:T(4,128)} add(f32[32,3,4,1024]{3,2,1,0:T(4,128)S(1)} %copy-done, f32[32,3,4,1024]{3,2,1,0:T(4,128)} %shard_map.109) | non-fusion elementwise | flops 393216 | bytes 4718592 | tf_op jit(solution)/shard_map/add | solution.py:645
Async XLA Ops:
  0.0 76.3 %copy-start = (f32[32,3,4,1024]{3,2,1,0:T(4,128)S(1)}, f32[32,3,4,1024]{3,2,1,0:T(4,128)}, u32[]{:S(2)}) copy-start(f32[32,3,4,1024]{3,2,1,0:T(4,128)} %feat_ref.1) | copy-start | bytes 4718596

commit v6 on v5

--- a/solution.py
+++ b/solution.py
@@ -522,7 +522,8 @@
         def write(g, carry):
             rows = pl.ds(pl.multiple_of(g * 8, 8), 8)
             two = jnp.concatenate([rows_out[k, rows] for k in range(8)], axis=1)
-            out_ref[pl.ds(g * 2, 2), z] = two.reshape(2, YR, XQ * QW)
+            two = two.reshape(2, YR, XQ * QW)
+            out_ref[pl.ds(g * 2, 2), z] = feat[z, pl.ds(g * 2, 2)] + two
             return carry
 
         lax.fori_loop(0, NP // 2, write, 0)
@@ -642,7 +643,7 @@
         jnp.swapaxes(tile_base, 2, 3),
         displacement,
     )
-    return features + added
+    return added
 
 
 def solution(mesh):

time: 79.7 us -> 79.1 us (level)
  other arithmetic: 3.21 us -> 0 us
  local copies, waits for them, and re-layouts: 0.01 us -> 2.67 us
    add x1 -> x0, other arithmetic: 3.21 us -> none  [body(): return features + added]
    unnamed x2 -> x1, local copies, waits for them, and re-layouts: 0.01 us -> 2.67 us
where the time goes in v6:
time: 79.1 us; the launch traced here: 78.9 us
  Pallas kernels  76.2 us (96%)
  local copies, waits for them, and re-layouts  2.67 us (3%)
    pallas_call x1, Pallas kernels, body(): pl.pallas_call(block_kernel, out_shape=jax.ShapeDtypeStruct(features.shap...  76.2 us
    unnamed x1, local copies, waits for them, and re-layouts  2.67 us

profile of v6, /device:TPU:1, one launch (start us, length us, event | category | flops | bytes accessed | tf_op | source)
XLA Modules:
  0.0 78.9 jit_solution(8140999329611817138)
XLA Ops:
  0.0 76.2 %shard_map.109 = f32[32,3,4,1024]{3,2,1,0:T(4,128)} custom-call(f32[32,3,4,1024]{3,2,1,0:T(4,128)} %feat_ref.1, f32[32,31]{1,0:T(8,128)} %xt_ref.1, f32[32,31]{1,0:T(8,128)} %yt_ref.1, bf16[32,128]{1,0:T(8,128)(2,1)} %bitcast.5, f32[1,128]{1,0:T(1,128)} %bitcast.7, bf16[32,128]{1,0:T(8,128)(2,1)} %project_ref.1, bf16[8,32,2048]{2,1,0:T(8,128)(2,1)} %atlas_ref.1, ...), custom_call_target="tpu_custom_call" | custom-call | flops 10000000000 | bytes 10000000 | tf_op jit(solution)/shard_map/pallas_call | solution.py:565
  76.2 2.7 %copy.13 = f32[32,3,4,1024]{3,2,1,0:T(4,128)} copy(f32[32,3,4,1024]{3,2,1,0:T(4,128)} %shard_map.109) | data formatting | bytes 3145728
